TPU v7x, 32 devices: a whole 2x2x4 slice. The times are simulated.
32 devices in a mesh: row: 4 (over x, core), col: 8 (over z, y).
Axes of the slice: x: 2, y: 2, z: 4, core: 2. Of those that a mesh axis runs over, the one named last changes fastest.
Arguments:
- object_field: float32 [2, 2048, 4096], P(None, 'row', 'col'), may hold values from -5 to 5
- probe: float32 [2, 2, 256, 256], replicated, may hold values from -5 to 5
- amplitudes: float32 [256, 256, 256], P(('row', 'col')), may hold values from 0 to 2.5
- positions: int32 [256, 2], P(('row', 'col')), may hold values from 0 to 3840, as said below
- counts: int32 [32], P(('row', 'col')), may hold values from 1 to 8, as said below
Outputs:
- new_object: float32 [2, 2048, 4096], P(None, 'row', 'col')
- new_probe: float32 [2, 2, 256, 256], replicated
Inputs may be any that keep to these rules, and one draw needn't show every extreme that they name: `positions`: each slot's patch lies inside the object, and its top-left pixel lies in the tile of the device that holds the slot. `counts`: one device holds exactly 8 live slots in every draw; the others fewer.
All inputs are finite; a program needn't handle non-finite values.
Results may differ from a plain program's by a relative error of at most 0.0003.
Values sent between devices are 32-bit elements; how exact they have to be, the bound alone decides.
No kernel may reach another device: no remote copies, remote signals or barrier semaphores. Data moves between devices by JAX's collectives and lax.ppermute only.
A program may use at most 256 MiB of HBM per device.

v0:
```python
import functools
import math

import jax
import jax.numpy as jnp
import ml_dtypes
import numpy as np
from jax import lax
from jax.experimental import pallas as pl
from jax.experimental.pallas import tpu as pltpu
from jax.sharding import PartitionSpec as P

F32 = jnp.float32
BF16 = jnp.bfloat16
MIB = 1024 * 1024
FLOOR = 0.3


def split_np(table):
    high = table.astype(ml_dtypes.bfloat16)
    low = (table - high.astype(np.float64)).astype(ml_dtypes.bfloat16)
    return high, low


def dft_tables(length):
    half = length // 2
    q = np.arange(half)[:, None]
    n = np.arange(half)[None, :]
    forward = []
    for odd in range(2):
        phase = (n * (2 * q + odd)) % length
        angle = phase * (-2.0 * math.pi / length)
        re = np.cos(angle) / math.sqrt(length)
        im = np.sin(angle) / math.sqrt(length)
        forward.append(np.stack(split_np(np.block([[re, -im], [im, re]]))))
    forward = np.stack(forward)
    return forward, np.ascontiguousarray(forward.transpose(0, 1, 3, 2))


def order_tables(length):
    order = np.concatenate([np.arange(0, length, 2), np.arange(1, length, 2)])
    table = np.eye(length)[order]
    rows = np.concatenate([table] * 3, axis=1)
    return rows.astype(ml_dtypes.bfloat16), rows.T.astype(ml_dtypes.bfloat16)


def dot(a, b):
    return jnp.dot(a, b, preferred_element_type=F32)


def split(x):
    high = x.astype(BF16)
    return high, (x - high.astype(F32)).astype(BF16)


def roll_rows(x, shift):
    return pltpu.roll(x.reshape(x.shape[0] // 8, 8, x.shape[1]), shift, 1)


def split_three(x):
    high = x.astype(BF16)
    rest = x - high.astype(F32)
    middle = rest.astype(BF16)
    return high, middle, (rest - middle.astype(F32)).astype(BF16)


def add_shifted(template, grid, where_t, where_g, top, left, size):
    top_s = top & 7
    top_b = pl.multiple_of(top - top_s, 8)
    left_s = left & 127
    left_b = pl.multiple_of(left - left_s, 128)
    step = 24
    wrapped = lax.broadcasted_iota(jnp.int32, (step, 128), 1) < left_s
    wrapped_rows = lax.broadcasted_iota(jnp.int32, (step // 8, 8, 128), 1) < top_s
    zero = jnp.zeros((step, 128), F32)
    blocks = size // 128
    for at in range(0, size + 8, step):
        parts = []
        for j in range(blocks):
            x = roll_rows(template[where_t + (pl.ds(at, step + 8), pl.ds(128 * j, 128))], top_s)
            x = jnp.where(wrapped_rows, x[:-1], x[1:]).reshape(step, 128)
            parts.append(pltpu.roll(x, left_s, 1))
        for j in range(blocks + 1):
            before = parts[j - 1] if j > 0 else zero
            after = parts[j] if j < blocks else zero
            spot = where_g + (pl.ds(top_b + at, step), pl.ds(left_b + 128 * j, 128))
            grid[spot] += jnp.where(wrapped, before, after)


def take_shifted(field, where, top, left, at, step, size):
    top_s = top & 7
    top_b = pl.multiple_of(top - top_s, 8)
    left_s = left & 127
    left_b = pl.multiple_of(left - left_s, 128)
    back = (128 - left_s) & 127
    keep = lax.broadcasted_iota(jnp.int32, (step + 8, 128), 1) < 128 - left_s
    keep_rows = lax.broadcasted_iota(jnp.int32, (step // 8, 8, 128), 1) < 8 - top_s
    blocks = size // 128
    parts = [
        pltpu.roll(field[where + (pl.ds(top_b + at, step + 8), pl.ds(left_b + 128 * j, 128))], back, 1)
        for j in range(blocks + 1)
    ]
    pieces = []
    for j in range(blocks):
        x = roll_rows(jnp.where(keep, parts[j], parts[j + 1]), (8 - top_s) & 7)
        pieces.append(jnp.where(keep_rows, x[:-1], x[1:]).reshape(step, 128))
    return jnp.concatenate(pieces, axis=1)


def light_kernel(meta, probe, inverse_light, template, grid):
    size = probe.shape[2]
    tile_rows, tile_cols = inverse_light.shape
    template[0:8, :] = jnp.zeros((8, size), F32)
    template[8 + size :, :] = jnp.zeros((8, size), F32)
    for at in range(0, size, 32):
        rows = pl.ds(at, 32)
        total = jnp.zeros((32, size), F32)
        for m in range(probe.shape[0]):
            total += probe[m, 0, rows] * probe[m, 0, rows] + probe[m, 1, rows] * probe[m, 1, rows]
        template[pl.ds(8 + at, 32), :] = total

    @pl.loop(0, tile_rows // 32)
    def _(step):
        rows = pl.ds(pl.multiple_of(size + step * 32, 32), 32)
        grid[rows, size : size + tile_cols] = jnp.zeros((32, tile_cols), F32)

    slots = meta.shape[1] // 2
    for device in range(4):

        @pl.loop(0, meta[device, 2 * slots])
        def _(slot):
            top = meta[device, 2 * slot] + size
            left = meta[device, 2 * slot + 1] + size

            @pl.when((top > 0) & (left > 0))
            def _():
                add_shifted(template, grid, (), (), top, left, size)

    @pl.loop(0, tile_rows // 32)
    def _(step):
        rows = pl.ds(pl.multiple_of(size + step * 32, 32), 32)
        out_rows = pl.ds(pl.multiple_of(step * 32, 32), 32)
        inverse_light[out_rows, :] = 1.0 / (grid[rows, size : size + tile_cols] + 1.0)


def light(meta, probe, tile_shape):
    size = probe.shape[2]
    vmem = pl.BlockSpec(memory_space=pltpu.VMEM)
    return pl.pallas_call(
        light_kernel,
        out_shape=jax.ShapeDtypeStruct(tile_shape, F32),
        in_specs=[pl.BlockSpec(memory_space=pltpu.SMEM), vmem],
        out_specs=vmem,
        scratch_shapes=[
            pltpu.VMEM((size + 16, size), F32),
            pltpu.VMEM((tile_shape[0] + 2 * size, tile_shape[1] + 2 * size), F32),
        ],
        compiler_params=pltpu.CompilerParams(vmem_limit_bytes=16 * MIB),
        cost_estimate=pl.CostEstimate(flops=4_000_000_000, bytes_accessed=16_000_000, transcendentals=0),
        name="light",
    )(meta, probe)


def arrange_kernel(meta, amplitudes, order_rows, order_cols, out):
    @pl.loop(0, meta[0, meta.shape[1] - 1])
    def _(slot):
        x = dot(order_rows[...], jnp.concatenate(split_three(amplitudes[slot]), axis=0))
        out[slot] = dot(jnp.concatenate(split_three(x), axis=1), order_cols[...])


def arrange(meta, amplitudes):
    order_rows, order_cols = (jnp.asarray(table) for table in order_tables(amplitudes.shape[2]))
    vmem = pl.BlockSpec(memory_space=pltpu.VMEM)
    return pl.pallas_call(
        arrange_kernel,
        out_shape=jax.ShapeDtypeStruct(amplitudes.shape, F32),
        in_specs=[pl.BlockSpec(memory_space=pltpu.SMEM)] + [vmem] * 3,
        out_specs=vmem,
        compiler_params=pltpu.CompilerParams(vmem_limit_bytes=16 * MIB),
        cost_estimate=pl.CostEstimate(flops=2_000_000_000, bytes_accessed=8_000_000, transcendentals=0),
        name="arrange",
    )(meta, amplitudes, order_rows, order_cols)


def three_left(table, t):
    return jnp.concatenate([table[t, 0], table[t, 0], table[t, 1]], axis=1)


def three_right(table, v):
    return jnp.concatenate([table[v, 0], table[v, 0], table[v, 1]], axis=0)


def weave(first, second):
    total = max(len(first), len(second))
    done = [0, 0]
    for i in range(1, total + 1):
        for k, pieces in enumerate((first, second)):
            while done[k] * total < i * len(pieces):
                pieces[done[k]]()
                done[k] += 1


def slots_kernel(
    needs_rim, meta, probe, amplitudes, sources, forward_t, backward_t, init, outs, probe_out,
    ext, grid, amp, chosen, patch_f, patch_b, x_f, y_f, z_f, g_s, x_b, z_b, back, template, sems,
):
    size = probe.shape[2]
    half = size // 2
    modes = probe.shape[0]
    slots = amplitudes.shape[0]
    tile_rows, tile_cols = (n - size for n in ext.shape[1:])
    step = 32
    load_sems, amp_sems, out_sems = sems

    regions = (
        (pl.ds(0, tile_rows), pl.ds(0, tile_cols)),
        (pl.ds(tile_rows, size), pl.ds(0, tile_cols)),
        (pl.ds(0, size), pl.ds(tile_cols, size)),
        (pl.ds(size, tile_rows - size), pl.ds(tile_cols, size)),
        (pl.ds(tile_rows, size), pl.ds(tile_cols, size)),
    )
    loads = [
        pltpu.make_async_copy(source, ext.at[:, rows, cols], load_sems.at[i])
        for i, (source, (rows, cols)) in enumerate(zip(sources, regions))
    ]
    if needs_rim:
        loads.append(pltpu.make_async_copy(init[0], grid.at[:, :, pl.ds(0, tile_cols)], load_sems.at[5]))
        loads.append(pltpu.make_async_copy(init[1], probe_out, load_sems.at[6]))
    for load in loads:
        load.start()

    def amp_copy(slot):
        return pltpu.make_async_copy(amplitudes.at[slot], amp.at[slot], amp_sems.at[slot])

    def choose(slot, found):
        beyond = meta[0, 2 * slot + 1] + size > tile_cols
        wanted = beyond if needs_rim else jnp.logical_not(beyond)

        @pl.when(wanted)
        def _():
            chosen[found] = slot
            amp_copy(slot).start()

        return found + wanted.astype(jnp.int32)

    count = lax.fori_loop(0, meta[0, 2 * slots], choose, jnp.zeros((), jnp.int32))

    @pl.loop(0, (tile_rows + size) // step)
    def _(at):
        rows = pl.ds(pl.multiple_of(at * step, step), step)
        for c in range(2):
            if needs_rim:
                grid[c, rows, tile_cols:] = jnp.zeros((step, size), F32)
            else:
                grid[c, rows, :] = jnp.zeros((step, tile_cols + size), F32)

    if not needs_rim:

        @pl.loop(0, size // step)
        def _(at):
            rows = pl.ds(pl.multiple_of(at * step, step), step)
            for c in range(2 * modes + 1):
                probe_out[c, rows, :] = jnp.zeros((step, size), F32)

    for c in range(2):
        template[c, 0:8, :] = jnp.zeros((8, size), F32)
        template[c, 8 + size :, :] = jnp.zeros((8, size), F32)
    for load in loads:
        load.wait()

    def corner(slot):
        return meta[0, 2 * slot], meta[0, 2 * slot + 1]

    def forward(slot):
        top, left = corner(slot)

        def take(at):
            rows = pl.ds(at, step)
            total = jnp.zeros((step, size), F32)
            for c in range(2):
                piece = take_shifted(ext, (c,), top, left, at, step, size)
                patch_f[c, rows, :] = piece
                total += piece * piece
            probe_out[2 * modes, rows, :] += total

        def fold_rows(m, at):
            cols = pl.ds(m * size, size)
            parts = []
            for base in (at, half + at):
                rows = pl.ds(base, step)
                pr, pi = patch_f[0, rows, :], patch_f[1, rows, :]
                qr, qi = probe[m, 0, rows, :], probe[m, 1, rows, :]
                parts.append((qr * pr - qi * pi, qr * pi + qi * pr))
            for c in range(2):
                rows = pl.ds(c * half + at, step)
                for t, value in enumerate((parts[0][c] + parts[1][c], parts[0][c] - parts[1][c])):
                    x_f[t, 0, rows, cols], x_f[t, 1, rows, cols] = split(value)

        def dft_rows(m, t):
            cols = pl.ds(m * size, size)
            high = x_f[t, 0, :, cols]
            u = dot(three_left(forward_t, t), jnp.concatenate([high, x_f[t, 1, :, cols], high], axis=0))
            rows = pl.ds(m * size + t * half, half)
            for v, value in enumerate((u[:, :half] + u[:, half:], u[:, :half] - u[:, half:])):
                high, low = split(value)
                for c in range(2):
                    lanes = pl.ds(c * half, half)
                    y_f[v, 0, rows, lanes] = high[c * half : (c + 1) * half]
                    y_f[v, 1, rows, lanes] = low[c * half : (c + 1) * half]

        def dft_cols(m, v):
            rows = pl.ds(m * size, size)
            high = y_f[v, 0, rows, :]
            z_f[v, rows, :] = dot(
                jnp.concatenate([high, y_f[v, 1, rows, :], high], axis=1), three_right(backward_t, v)
            )

        def scale(v, at):
            if v == 0 and at == 0:
                amp_copy(slot).wait()
            waves = [z_f[v, pl.ds(m * size + at, step), :] for m in range(modes)]
            total = jnp.zeros((step, half), F32)
            for wave in waves:
                total += wave[:, :half] * wave[:, :half] + wave[:, half:] * wave[:, half:]
            measured = amp[slot, pl.ds(at, step), pl.ds(v * half, half)]
            factor = measured * lax.rsqrt(jnp.maximum(total, FLOOR * FLOOR)) - 1.0
            factor = jnp.concatenate([factor, factor], axis=1)
            for m in range(modes):
                rows = pl.ds(m * size + at, step)
                g_s[v, 0, rows, :], g_s[v, 1, rows, :] = split(waves[m] * factor)

        pieces = [(take, at) for at in range(0, size, step)]
        for m in range(modes):
            pieces += [(fold_rows, m, at) for at in range(0, half, step)]
            pieces += [(dft_rows, m, t) for t in range(2)]
            pieces += [(dft_cols, m, v) for v in range(2)]
        pieces += [(scale, v, at) for v in range(2) for at in range(0, size, step)]
        return [functools.partial(*piece) for piece in pieces]

    def backward(slot):
        top, left = corner(slot)

        def dft_cols(m, v):
            rows = pl.ds(m * size, size)
            high = g_s[v, 0, rows, :]
            z_b[v, rows, :] = dot(
                jnp.concatenate([high, g_s[v, 1, rows, :], high], axis=1), three_right(forward_t, v)
            )

        def unfold_cols(m, t, at):
            rows = pl.ds(m * size + t * half + at, step)
            even, odd = z_b[0, rows, :], z_b[1, rows, :]
            for v, value in enumerate((even + odd, even - odd)):
                high, low = split(value)
                cols = pl.ds(m * size + v * half, half)
                for c in range(2):
                    spot = pl.ds(c * half + at, step)
                    x_b[t, 0, spot, cols] = high[:, c * half : (c + 1) * half]
                    x_b[t, 1, spot, cols] = low[:, c * half : (c + 1) * half]

        def dft_rows(m, t):
            cols = pl.ds(m * size, size)
            high = x_b[t, 0, :, cols]
            back[m, t] = dot(three_left(backward_t, t), jnp.concatenate([high, x_b[t, 1, :, cols], high], axis=0))

        def gradients(at):
            waves = []
            for m in range(modes):
                pair = []
                for c in range(2):
                    rows = pl.ds(c * half + at, step)
                    even, odd = back[m, 0, rows, :], back[m, 1, rows, :]
                    pair.append((even + odd, even - odd))
                waves.append(pair)
            for h in range(2):
                rows = pl.ds(h * half + at, step)
                pr, pi = patch_b[0, rows, :], patch_b[1, rows, :]
                grad_r = jnp.zeros((step, size), F32)
                grad_i = jnp.zeros((step, size), F32)
                for m in range(modes):
                    br, bi = waves[m][0][h], waves[m][1][h]
                    qr, qi = probe[m, 0, rows, :], probe[m, 1, rows, :]
                    grad_r += qr * br + qi * bi
                    grad_i += qr * bi - qi * br
                    probe_out[2 * m, rows, :] += pr * br + pi * bi
                    probe_out[2 * m + 1, rows, :] += pr * bi - pi * br
                spot = pl.ds(8 + h * half + at, step)
                template[0, spot, :] = grad_r
                template[1, spot, :] = grad_i

        def add(c):
            add_shifted(template, grid, (c,), (c,), top, left, size)

        pieces = []
        for m in range(modes):
            pieces += [(dft_cols, m, v) for v in range(2)]
        for m in range(modes):
            pieces += [(unfold_cols, m, t, at) for t in range(2) for at in range(0, half, step)]
            pieces += [(dft_rows, m, t) for t in range(2)]
        pieces += [(gradients, at) for at in range(0, half, step)]
        pieces += [(add, c) for c in range(2)]
        return [functools.partial(*piece) for piece in pieces]

    def hand_over():
        for at in range(0, size, step):
            for c in range(2):
                patch_b[c, pl.ds(at, step), :] = patch_f[c, pl.ds(at, step), :]

    @pl.when(count > 0)
    def _():
        weave(forward(chosen[0]), [])
        hand_over()

        def visit(index, _):
            weave(backward(chosen[index]), forward(chosen[index + 1]))
            hand_over()
            return 0

        lax.fori_loop(0, count - 1, visit, 0)
        weave(backward(chosen[count - 1]), [])

    if needs_rim:
        parts = [
            grid.at[:, pl.ds(0, tile_rows), pl.ds(0, tile_cols)],
            grid.at[:, pl.ds(0, tile_rows), pl.ds(tile_cols, size)],
            grid.at[:, pl.ds(tile_rows, size), pl.ds(0, tile_cols)],
            grid.at[:, pl.ds(tile_rows, size), pl.ds(tile_cols, size)],
        ]
    else:
        parts = [grid.at[:, :, pl.ds(0, tile_cols)]]
    stores = [pltpu.make_async_copy(part, out, out_sems.at[i]) for i, (part, out) in enumerate(zip(parts, outs))]
    for store in stores:
        store.start()
    for store in stores:
        store.wait()


def visit_slots(meta, probe, amplitudes, sources, init):
    size = probe.shape[2]
    modes = probe.shape[0]
    slots = amplitudes.shape[0]
    rows, cols = sources[0].shape[1:]
    tables = [jnp.asarray(item) for item in dft_tables(size)]
    vmem = pl.BlockSpec(memory_space=pltpu.VMEM)
    anywhere = pl.BlockSpec(memory_space=pl.ANY)
    needs_rim = bool(init)
    if needs_rim:
        shapes = [(2, rows, cols), (2, rows, size), (2, size, cols), (2, size, size)]
    else:
        shapes = [(2, rows + size, cols)]
    splits = np.cumsum([1, 1, 1, len(sources), 1, 1, len(init), len(shapes), 1])

    def kernel(*refs):
        meta, probe, amplitudes, sources, forward_t, backward_t, init, outs, probe_out = (
            refs[a:b] for a, b in zip([0, *splits[:-1]], splits)
        )
        scratch = refs[splits[-1] :]
        slots_kernel(
            needs_rim, meta[0], probe[0], amplitudes[0], sources, forward_t[0], backward_t[0], init, outs,
            probe_out[0], *scratch[:-3], scratch[-3:],
        )

    return pl.pallas_call(
        kernel,
        out_shape=[jax.ShapeDtypeStruct(shape, F32) for shape in shapes]
        + [jax.ShapeDtypeStruct((2 * modes + 1, size, size), F32)],
        in_specs=[pl.BlockSpec(memory_space=pltpu.SMEM), vmem] + [anywhere] * (1 + len(sources))
        + [vmem] * 2 + [anywhere] * len(init),
        out_specs=[anywhere] * len(shapes) + [vmem],
        scratch_shapes=[
            pltpu.VMEM((2, rows + size, cols + size), F32),
            pltpu.VMEM((2, rows + size, cols + size), F32),
            pltpu.VMEM(amplitudes.shape, F32),
            pltpu.SMEM((slots,), jnp.int32),
            pltpu.VMEM((2, size, size), F32),
            pltpu.VMEM((2, size, size), F32),
            pltpu.VMEM((2, 2, size, modes * size), BF16),
            pltpu.VMEM((2, 2, modes * size, size), BF16),
            pltpu.VMEM((2, modes * size, size), F32),
            pltpu.VMEM((2, 2, modes * size, size), BF16),
            pltpu.VMEM((2, 2, size, modes * size), BF16),
            pltpu.VMEM((2, modes * size, size), F32),
            pltpu.VMEM((modes, 2, size, size), F32),
            pltpu.VMEM((2, size + 16, size), F32),
            pltpu.SemaphoreType.DMA((7,)),
            pltpu.SemaphoreType.DMA((slots,)),
            pltpu.SemaphoreType.DMA((4,)),
        ],
        compiler_params=pltpu.CompilerParams(vmem_limit_bytes=32 * MIB),
        cost_estimate=pl.CostEstimate(flops=12_000_000_000, bytes_accessed=16_000_000, transcendentals=0),
        name="slots_beyond" if needs_rim else "slots_inside",
    )(meta, probe, amplitudes, *sources, *tables, *init)


def finish_kernel(own, right, lower, corner, inverse_light, tile, out):
    size = right.shape[2]
    step = pl.program_id(0)
    scale = inverse_light[...]
    spill = jnp.where(step < size // own.shape[1], 1.0, 0.0)
    for c in range(2):
        near = own[c, :, :size] + right[c] + spill * (lower[c, :, :size] + corner[c])
        far = own[c, :, size:] + spill * lower[c, :, size:]
        out[c, :, :size] = tile[c, :, :size] + near * scale[:, :size]
        out[c, :, size:] = tile[c, :, size:] + far * scale[:, size:]


def finish(own, right, lower, corner, inverse_light, tile):
    rows, cols = tile.shape[1:]
    size = right.shape[2]
    block = 128
    last = size // block - 1
    whole = pl.BlockSpec((2, block, cols), lambda i: (0, i, 0))
    return pl.pallas_call(
        finish_kernel,
        grid=(rows // block,),
        out_shape=jax.ShapeDtypeStruct(tile.shape, F32),
        in_specs=[
            whole,
            pl.BlockSpec((2, block, size), lambda i: (0, i, 0)),
            pl.BlockSpec((2, block, cols), lambda i: (0, jnp.minimum(i, last), 0)),
            pl.BlockSpec((2, block, size), lambda i: (0, jnp.minimum(i, last), 0)),
            pl.BlockSpec((block, cols), lambda i: (i, 0)),
            whole,
        ],
        out_specs=whole,
        cost_estimate=pl.CostEstimate(flops=3_000_000, bytes_accessed=12_000_000, transcendentals=0),
        name="finish",
    )(own, right, lower, corner, inverse_light, tile)


def from_behind(array, axis, by):
    count = lax.axis_size(axis)
    pairs = [(i, i + by) for i in range(count) if 0 <= i + by < count]
    return lax.ppermute(array, axis, pairs)


def exchange(array, axis, bit):
    count = lax.axis_size(axis)
    return lax.ppermute(array, axis, [(i, i ^ bit) for i in range(count)])


def together(*arrays):
    return lax.optimization_barrier(arrays)


def body(object_field, probe, amplitudes, positions, counts):
    modes, _, size, _ = probe.shape
    tile_rows, tile_cols = object_field.shape[1:]
    slots = amplitudes.shape[0]
    origin = jnp.stack([lax.axis_index("row") * tile_rows, lax.axis_index("col") * tile_cols]).astype(jnp.int32)

    def relative(table):
        return jnp.concatenate([table[:, : 2 * slots] - jnp.tile(origin, slots)[None], table[:, 2 * slots :]], axis=1)

    meta = jnp.concatenate([positions.reshape(1, 2 * slots), counts.reshape(1, 1)], axis=1)
    mine = relative(meta)

    right_up = from_behind(object_field[:, :size, :size], "col", -1)
    lower = from_behind(object_field[:, :size, :], "row", -1)
    amplitudes = arrange(mine, amplitudes)
    right_up, amplitudes, rest = together(right_up, amplitudes, object_field[:, size:, :size])
    corner = from_behind(right_up, "row", -1)
    right_down = from_behind(rest, "col", -1)
    init = visit_slots(mine, probe, amplitudes, [object_field, lower], [])
    right_up, right_down, corner, *init = together(right_up, right_down, corner, *init)
    own, right_spill, lower_spill, corner_spill, sums = visit_slots(
        mine, probe, amplitudes, [object_field, lower, right_up, right_down, corner], list(init)
    )
    corner_spill = from_behind(corner_spill, "row", 1)
    right_spill = from_behind(right_spill, "col", 1)
    lower_spill = from_behind(lower_spill, "row", 1)

    share = sums
    start = jnp.zeros((), jnp.int32)
    bits = [1 << k for k in range(lax.axis_size("row").bit_length() - 1)]
    inverse_light = None
    for bit in bits:
        half = share.shape[1] // 2
        upper = (lax.axis_index("row") // bit) % 2
        keep = lax.dynamic_slice_in_dim(share, upper * half, half, axis=1)
        send = lax.dynamic_slice_in_dim(share, (1 - upper) * half, half, axis=1)
        got = exchange(send, "row", bit)
        if bit == bits[-1]:
            meta, keep = together(meta, keep)
            table = jnp.concatenate([meta, from_behind(meta, "col", 1)], axis=0)
            table = jnp.concatenate([table, from_behind(table, "row", 1)], axis=0)
            inverse_light = light(relative(table), probe, (tile_rows, tile_cols))
            got, inverse_light = together(got, inverse_light)
        share = keep + got
        start = start + upper * half
    parts = lax.axis_size("col")
    rows = share.shape[1] // parts
    share = share.reshape(2 * modes + 1, parts, rows, size).transpose(1, 0, 2, 3)
    share = lax.all_to_all(share, "col", 0, 0, tiled=True).sum(axis=0)
    old = lax.dynamic_slice_in_dim(
        probe.reshape(2 * modes, size, size), start + lax.axis_index("col") * rows, rows, axis=1
    )
    new = old + share[: 2 * modes] / (share[2 * modes :] + 1.0)
    new = jnp.broadcast_to(new[None], (parts,) + new.shape)
    new = lax.all_to_all(new, "col", 0, 0, tiled=True)
    new = new.transpose(1, 0, 2, 3).reshape(2 * modes, parts * rows, size)
    new, corner_spill, right_spill, lower_spill = together(new, corner_spill, right_spill, lower_spill)
    corner_spill = from_behind(corner_spill, "col", 1)
    for bit in reversed(bits):
        upper = (lax.axis_index("row") // bit) % 2 == 1
        other = exchange(new, "row", bit)
        if bit == bits[-1]:
            new_object = finish(own, right_spill, lower_spill, corner_spill, inverse_light, object_field)
            other, new_object = together(other, new_object)
        new = jnp.concatenate([jnp.where(upper, other, new), jnp.where(upper, new, other)], axis=1)
    return (new_object, new.reshape(modes, 2, size, size))


def solution(mesh):
    in_specs = (
        P(None, "row", "col"),
        P(),
        P(("row", "col"), None, None),
        P(("row", "col"), None),
        P(("row", "col")),
    )
    out_specs = (P(None, "row", "col"), P())
    return jax.shard_map(body, mesh=mesh, in_specs=in_specs, out_specs=out_specs, check_vma=False)
```

profile of v0, /device:TPU:17, one launch (start us, length us, event | category | flops | bytes accessed | tf_op | source)
XLA Modules:
  0.0 156.0 jit_solution(2494327966092071584)
XLA Ops:
  0.7 2.4 %slice.23 = f32[2,256,512]{2,1,0:T(8,128)} slice(f32[2,512,512]{2,1,0:T(8,128)} %tile.4), slice={[0:2], [0:256], [0:512]} | slice | bytes 2097152 | tf_op jit(solution)/shard_map/slice | solution.py:559
  3.1 2.6 %collective-permute-start.1 = (f32[2,256,512]{2,1,0:T(8,128)}, f32[2,256,512]{2,1,0:T(8,128)S(1)}, u32[]{:S(2)}, u32[]{:S(2)}) collective-permute-start(f32[2,256,512]{2,1,0:T(8,128)} %slice.23), channel_id=1, source_target_pairs={{8,0},{16,8},{24,16},{9,1},{17,9},{25,17},{10,2},{18,10},{26,18},{... | collective-permute-start | bytes 3145736 | tf_op jit(solution)/shard_map/ppermute | solution.py:534
  5.7 1.1 fusion.2
  6.7 3.0 %collective-permute-start = (f32[2,256,256]{2,1,0:T(8,128)}, f32[2,256,256]{2,1,0:T(8,128)}, u32[]{:S(2)}, u32[]{:S(2)}) collective-permute-start(f32[2,256,256]{2,1,0:T(8,128)} %get-tuple-element.53), channel_id=1, source_target_pairs={{1,0},{2,1},{3,2},{4,3},{5,4},{6,5},{7,6},{9,8},{10,9},{11,10},{12... | collective-permute-start | bytes 1572872 | tf_op jit(solution)/shard_map/ppermute | solution.py:534
  10.9 1.6 %copy-done.5 = f32[8,256,256]{2,1,0:T(8,128)S(1)} copy-done((f32[8,256,256]{2,1,0:T(8,128)S(1)}, f32[8,256,256]{2,1,0:T(8,128)}, u32[]{:S(2)}) %copy-start.5) | copy-done | bytes 2097176
  13.5 1.8 %arrange.1.refs_2_ = f32[8,256,256]{2,1,0:T(8,128)S(1)} custom-call(s32[1,17]{1,0:T(1,128)S(1)} %pad_add_fusion.5.meta.refs_0_, f32[8,256,256]{2,1,0:T(8,128)S(1)} %copy-done.5, bf16[256,768]{1,0:T(8,128)(2,1)S(1)} %copy-done.16, bf16[768,256]{1,0:T(8,128)(2,1)S(1)} %copy-done.15), custom_call_target="tpu_custom_call" | custom-call | flops 2000000000 | bytes 8000000 | tf_op jit(solution)/shard_map/arrange/pallas_call | solution.py:174
  15.2 7.3 %collective-permute-done.refs_5_ = f32[2,256,256]{2,1,0:T(8,128)} collective-permute-done((f32[2,256,256]{2,1,0:T(8,128)}, f32[2,256,256]{2,1,0:T(8,128)}, u32[]{:S(2)}, u32[]{:S(2)}) %collective-permute-start) | collective-permute-done | bytes 524320 | tf_op jit(solution)/shard_map/ppermute | solution.py:534
  22.6 3.9 %collective-permute-start.2 = (f32[2,256,256]{2,1,0:T(8,128)S(1)}, f32[2,256,256]{2,1,0:T(8,128)S(1)}, u32[]{:S(2)}, u32[]{:S(2)}) collective-permute-start(f32[2,256,256]{2,1,0:T(8,128)S(1)} %copy-done.18), channel_id=1, source_target_pairs={{1,0},{2,1},{3,2},{4,3},{5,4},{6,5},{7,6},{9,8},{10,9},{11,10},{12... | collective-permute-start | bytes 1572872 | tf_op jit(solution)/shard_map/ppermute | solution.py:534
  26.5 2.6 %collective-permute-start.3 = (f32[2,256,256]{2,1,0:T(8,128)}, f32[2,256,256]{2,1,0:T(8,128)S(1)}, u32[]{:S(2)}, u32[]{:S(2)}) collective-permute-start(f32[2,256,256]{2,1,0:T(8,128)} %collective-permute-done.refs_5_), channel_id=1, source_target_pairs={{8,0},{16,8},{24,16},{9,1},{17,9},{25,17},{10,2},{18,10},{26,18},{... | collective-permute-start | bytes 1572872 | tf_op jit(solution)/shard_map/ppermute | solution.py:534
  29.1 2.1 %slots_inside.1 = (f32[2,768,512]{2,1,0:T(8,128)S(1)}, f32[5,256,256]{2,1,0:T(8,128)S(1)}) custom-call(s32[1,17]{1,0:T(1,128)S(1)} %pad_add_fusion.5.meta.refs_0_, f32[2,2,256,256]{3,2,1,0:T(8,128)S(1)} %copy-done.3, f32[8,256,256]{2,1,0:T(8,128)S(1)} %arrange.1.refs_2_, f32[2,512,512]{2,1,0:T(8,128)S(1)} %copy-done, ...), custom_call_target="tpu_custom_call" | custom-call | flops 12000000000 | bytes 16000000 | tf_op jit(solution)/shard_map/slots_inside/pallas_call | solution.py:463
  31.2 7.4 %collective-permute-done.2.refs_6_ = f32[2,256,256]{2,1,0:T(8,128)S(1)} collective-permute-done((f32[2,256,256]{2,1,0:T(8,128)S(1)}, f32[2,256,256]{2,1,0:T(8,128)S(1)}, u32[]{:S(2)}, u32[]{:S(2)}) %collective-permute-start.2) | collective-permute-done | bytes 524320 | tf_op jit(solution)/shard_map/ppermute | solution.py:534
  38.6 1.2 copy-done.11
  39.8 10.1 %slots_beyond.1 = (f32[2,512,512]{2,1,0:T(8,128)S(1)}, f32[2,512,256]{2,1,0:T(8,128)S(1)}, f32[2,256,512]{2,1,0:T(8,128)S(1)}, f32[2,256,256]{2,1,0:T(8,128)S(1)}, f32[5,256,256]{2,1,0:T(8,128)S(1)}) custom-call(s32[1,17]{1,0:T(1,128)S(1)} %pad_add_fusion.5.meta.refs_0_, f32[2,2,256,256]{3,2,1,0:T(8,128)S(1)} %copy-done.3, ...), custom_call_target="tpu_custom_call" | custom-call | flops 12000000000 | bytes 16000000 | tf_op jit(solution)/shard_map/slots_beyond/pallas_call | solution.py:463
  49.9 1.4 copy-done.1
  54.2 2.1 %collective-permute-done.4 = f32[5,128,256]{2,1,0:T(8,128)} collective-permute-done((f32[5,128,256]{2,1,0:T(8,128)S(1)}, f32[5,128,256]{2,1,0:T(8,128)}, u32[]{:S(2)}, u32[]{:S(2)}) %collective-permute-start.4) | collective-permute-done | bytes 655392 | tf_op jit(solution)/shard_map/ppermute | solution.py:539
  56.3 1.2 dynamic-slice_add_fusion
  58.3 1.9 %collective-permute-start.6 = (s32[1,17]{1,0:T(1,128)S(1)}, s32[1,17]{1,0:T(1,128)S(1)}, u32[]{:S(2)}, u32[]{:S(2)}) collective-permute-start(s32[1,17]{1,0:T(1,128)S(1)} %pad_add_fusion.3), channel_id=1, source_target_pairs={{0,1},{1,2},{2,3},{3,4},{4,5},{5,6},{6,7},{8,9},{9,10},{10,11},{11... | collective-permute-start | bytes 212 | tf_op jit(solution)/shard_map/ppermute | solution.py:534
  60.3 3.2 %collective-permute-done.6 = s32[1,17]{1,0:T(1,128)S(1)} collective-permute-done((s32[1,17]{1,0:T(1,128)S(1)}, s32[1,17]{1,0:T(1,128)S(1)}, u32[]{:S(2)}, u32[]{:S(2)}) %collective-permute-start.6) | collective-permute-done | bytes 100 | tf_op jit(solution)/shard_map/ppermute | solution.py:534
  63.5 5.1 %collective-permute-start.7 = (s32[2,17]{1,0:T(2,128)S(1)}, s32[2,17]{1,0:T(2,128)S(1)}, u32[]{:S(2)}, u32[]{:S(2)}) collective-permute-start(s32[2,17]{1,0:T(2,128)S(1)} %pad_add_fusion.2), channel_id=1, source_target_pairs={{0,8},{8,16},{16,24},{1,9},{9,17},{17,25},{2,10},{10,18},{18,26},{... | collective-permute-start | bytes 416 | tf_op jit(solution)/shard_map/ppermute | solution.py:534
  69.5 2.2 %light.1.inverse_light = f32[512,512]{1,0:T(8,128)S(1)} custom-call(s32[4,17]{1,0:T(4,128)S(1)} %pad_add_fusion.1.meta, f32[2,2,256,256]{3,2,1,0:T(8,128)S(1)} %copy-done.4), custom_call_target="tpu_custom_call" | custom-call | flops 4000000000 | bytes 16000000 | tf_op jit(solution)/shard_map/light/pallas_call | solution.py:149
  72.7 4.5 %collective-permute-done.5 = f32[5,64,256]{2,1,0:T(8,128)S(1)} collective-permute-done((f32[5,64,256]{2,1,0:T(8,128)}, f32[5,64,256]{2,1,0:T(8,128)S(1)}, u32[]{:S(2)}, u32[]{:S(2)}) %collective-permute-start.5) | collective-permute-done | bytes 327712 | tf_op jit(solution)/shard_map/ppermute | solution.py:539
  77.9 15.2 %all-to-all-start = ((f32[8,5,8,256]{3,2,1,0:T(8,128)}), f32[8,5,8,256]{3,2,1,0:T(8,128)S(1)}, u32[]{:S(2)}, u32[]{:S(2)}) async-start(f32[8,5,8,256]{3,2,1,0:T(8,128)} %copy_bitcast_fusion), calls=%async_computation | async-start | bytes 655360 | tf_op jit(solution)/shard_map/all_to_all | solution.py:594
  93.2 3.1 %collective-permute-start.9 = (f32[2,512,256]{2,1,0:T(8,128)S(1)}, f32[2,512,256]{2,1,0:T(8,128)}, u32[]{:S(2)}, u32[]{:S(2)}) collective-permute-start(f32[2,512,256]{2,1,0:T(8,128)S(1)} %copy-done.9), channel_id=1, source_target_pairs={{0,1},{1,2},{2,3},{3,4},{4,5},{5,6},{6,7},{8,9},{9,10},{10,11},{11... | collective-permute-start | bytes 3145736 | tf_op jit(solution)/shard_map/ppermute | solution.py:534
  96.3 4.2 %collective-permute-start.10 = (f32[2,256,512]{2,1,0:T(8,128)S(1)}, f32[2,256,512]{2,1,0:T(8,128)}, u32[]{:S(2)}, u32[]{:S(2)}) collective-permute-start(f32[2,256,512]{2,1,0:T(8,128)S(1)} %copy-done.7), channel_id=1, source_target_pairs={{0,8},{8,16},{16,24},{1,9},{9,17},{17,25},{2,10},{10,18},{18,26},{... | collective-permute-start | bytes 3145736 | tf_op jit(solution)/shard_map/ppermute | solution.py:534
  100.5 1.9 %collective-permute-start.8 = (f32[2,256,256]{2,1,0:T(8,128)}, f32[2,256,256]{2,1,0:T(8,128)}, u32[]{:S(2)}, u32[]{:S(2)}) collective-permute-start(f32[2,256,256]{2,1,0:T(8,128)} %copy-done.12), channel_id=1, source_target_pairs={{0,8},{8,16},{16,24},{1,9},{9,17},{17,25},{2,10},{10,18},{18,26},{... | collective-permute-start | bytes 1572872 | tf_op jit(solution)/shard_map/ppermute | solution.py:534
  102.5 27.4 %all_to_all.10 = f32[8,4,8,256]{3,2,1,0:T(8,128)S(1)} all-to-all(f32[8,4,8,256]{3,2,1,0:T(8,128)S(1)} %broadcast_in_dim.2), channel_id=1, replica_groups=mesh['row'=4,'col'=8] {'col'}, dimensions={0} | all-to-all | bytes 524288 | tf_op jit(solution)/shard_map/all_to_all | solution.py:600
  129.9 1.9 %collective-permute-start.12 = (f32[2,256,256]{2,1,0:T(8,128)}, f32[2,256,256]{2,1,0:T(8,128)S(1)}, u32[]{:S(2)}, u32[]{:S(2)}) collective-permute-start(f32[2,256,256]{2,1,0:T(8,128)} %collective-permute-done.8), channel_id=1, source_target_pairs={{0,1},{1,2},{2,3},{3,4},{4,5},{5,6},{6,7},{8,9},{9,10},{10,11},{11... | collective-permute-start | bytes 1572872 | tf_op jit(solution)/shard_map/ppermute | solution.py:534
  132.3 12.2 %collective-permute-done.12.corner = f32[2,256,256]{2,1,0:T(8,128)S(1)} collective-permute-done((f32[2,256,256]{2,1,0:T(8,128)}, f32[2,256,256]{2,1,0:T(8,128)S(1)}, u32[]{:S(2)}, u32[]{:S(2)}) %collective-permute-start.12) | collective-permute-done | bytes 524320 | tf_op jit(solution)/shard_map/ppermute | solution.py:534
  145.4 5.1 %finish.1 = f32[2,512,512]{2,1,0:T(8,128)} custom-call(f32[2,512,512]{2,1,0:T(8,128)} %copy-done.1, f32[2,512,256]{2,1,0:T(8,128)} %collective-permute-done.9.right, f32[2,256,512]{2,1,0:T(8,128)} %collective-permute-done.10.lower, f32[2,256,256]{2,1,0:T(8,128)} %copy-done.17, f32[512,512]{1,0:T(8,128)} %copy-done.2, f32[2,512,512]{2,1,0:T(8,128)} %tile.4), custom_call_target="tpu_custom_call" | custom-call | flops 3000000 | bytes 12000000 | tf_op jit(solution)/shard_map/finish/pallas_call | solution.py:513
  150.5 2.8 %collective-permute-start.13 = (f32[4,128,256]{2,1,0:T(8,128)S(1)}, f32[4,128,256]{2,1,0:T(8,128)S(1)}, u32[]{:S(2)}, u32[]{:S(2)}) collective-permute-start(f32[4,128,256]{2,1,0:T(8,128)S(1)} %pad_maximum_fusion.1), channel_id=1, source_target_pairs={{0,8},{8,0},{16,24},{24,16},{1,9},{9,1},{17,25},{25,17},{2,10},{10... | collective-permute-start | bytes 1572872 | tf_op jit(solution)/shard_map/ppermute | solution.py:539
  153.3 1.5 collective-permute-done.13
  155.0 1.0 pad_maximum_fusion
  (73 shorter events, 9.4 us)
Async XLA Ops:
  0.6 5.0 %copy-start = (f32[2,512,512]{2,1,0:T(8,128)S(1)}, f32[2,512,512]{2,1,0:T(8,128)}, u32[]{:S(2)}) copy-start(f32[2,512,512]{2,1,0:T(8,128)} %tile.4) | copy-start | bytes 6291460
  0.6 10.2 %copy-start.15 = (bf16[768,256]{1,0:T(8,128)(2,1)S(1)}, bf16[768,256]{1,0:T(8,128)(2,1)}, u32[]{:S(2)}) copy-start(bf16[768,256]{1,0:T(8,128)(2,1)} %constant.77.clone.order_cols) | copy-start | bytes 1179652
  0.7 9.9 %copy-start.19 = (s32[8,2]{0,1:T(2,128)S(1)}, s32[8,2]{0,1:T(2,128)}, u32[]{:S(2)}) copy-start(s32[8,2]{0,1:T(2,128)} %param.14) | copy-start | bytes 196
  3.1 26.0 %collective-permute-start.1 = (f32[2,256,512]{2,1,0:T(8,128)}, f32[2,256,512]{2,1,0:T(8,128)S(1)}, u32[]{:S(2)}, u32[]{:S(2)}) collective-permute-start(f32[2,256,512]{2,1,0:T(8,128)} %slice.23), channel_id=1, source_target_pairs={{8,0},{16,8},{24,16},{9,1},{17,9},{25,17},{10,2},{18,10},{26,18},{... | collective-permute-start | bytes 3145736 | tf_op jit(solution)/shard_map/ppermute | solution.py:534
  6.7 15.8 %collective-permute-start = (f32[2,256,256]{2,1,0:T(8,128)}, f32[2,256,256]{2,1,0:T(8,128)}, u32[]{:S(2)}, u32[]{:S(2)}) collective-permute-start(f32[2,256,256]{2,1,0:T(8,128)} %get-tuple-element.53), channel_id=1, source_target_pairs={{1,0},{2,1},{3,2},{4,3},{5,4},{6,5},{7,6},{9,8},{10,9},{11,10},{12... | collective-permute-start | bytes 1572872 | tf_op jit(solution)/shard_map/ppermute | solution.py:534
  10.9 1.6 %copy-start.5 = (f32[8,256,256]{2,1,0:T(8,128)S(1)}, f32[8,256,256]{2,1,0:T(8,128)}, u32[]{:S(2)}) copy-start(f32[8,256,256]{2,1,0:T(8,128)} %amplitudes.1) | copy-start | bytes 6291460
  12.5 1.0 copy-start.16
  13.5 9.1 %copy-start.18 = (f32[2,256,256]{2,1,0:T(8,128)S(1)}, f32[2,256,256]{2,1,0:T(8,128)}, u32[]{:S(2)}) copy-start(f32[2,256,256]{2,1,0:T(8,128)} %get-tuple-element.29) | copy-start | bytes 1572868
  13.5 15.7 %copy-start.3 = (f32[2,2,256,256]{3,2,1,0:T(8,128)S(1)}, f32[2,2,256,256]{3,2,1,0:T(8,128)}, u32[]{:S(2)}) copy-start(f32[2,2,256,256]{3,2,1,0:T(8,128)} %probe.1) | copy-start | bytes 3145732
  13.5 15.7 %copy-start.13 = (bf16[2,2,256,256]{3,2,1,0:T(8,128)(2,1)S(1)}, bf16[2,2,256,256]{3,2,1,0:T(8,128)(2,1)}, u32[]{:S(2)}) copy-start(bf16[2,2,256,256]{3,2,1,0:T(8,128)(2,1)} %constant.79.clone.refs_6_.refs_9_) | copy-start | bytes 1572868
  13.5 15.7 %copy-start.14 = (bf16[2,2,256,256]{3,2,1,0:T(8,128)(2,1)S(1)}, bf16[2,2,256,256]{3,2,1,0:T(8,128)(2,1)}, u32[]{:S(2)}) copy-start(bf16[2,2,256,256]{3,2,1,0:T(8,128)(2,1)} %constant.78.clone.refs_5_.refs_8_) | copy-start | bytes 1572868
  22.6 16.0 %collective-permute-start.2 = (f32[2,256,256]{2,1,0:T(8,128)S(1)}, f32[2,256,256]{2,1,0:T(8,128)S(1)}, u32[]{:S(2)}, u32[]{:S(2)}) collective-permute-start(f32[2,256,256]{2,1,0:T(8,128)S(1)} %copy-done.18), channel_id=1, source_target_pairs={{1,0},{2,1},{3,2},{4,3},{5,4},{6,5},{7,6},{9,8},{10,9},{11,10},{12... | collective-permute-start | bytes 1572872 | tf_op jit(solution)/shard_map/ppermute | solution.py:534
  26.5 12.1 %collective-permute-start.3 = (f32[2,256,256]{2,1,0:T(8,128)}, f32[2,256,256]{2,1,0:T(8,128)S(1)}, u32[]{:S(2)}, u32[]{:S(2)}) collective-permute-start(f32[2,256,256]{2,1,0:T(8,128)} %collective-permute-done.refs_5_), channel_id=1, source_target_pairs={{8,0},{16,8},{24,16},{9,1},{17,9},{25,17},{10,2},{18,10},{26,18},{... | collective-permute-start | bytes 1572872 | tf_op jit(solution)/shard_map/ppermute | solution.py:534
  29.1 2.1 %copy-start.10 = (f32[2,256,512]{2,1,0:T(8,128)}, f32[2,256,512]{2,1,0:T(8,128)S(1)}, u32[]{:S(2)}) copy-start(f32[2,256,512]{2,1,0:T(8,128)S(1)} %collective-permute-done.1.refs_4_) | copy-start | bytes 3145732
  38.6 1.2 copy-start.11
  49.9 1.4 copy-start.1
  51.2 1.0 copy-start.6
  54.0 15.5 %copy-start.4 = (f32[2,2,256,256]{3,2,1,0:T(8,128)S(1)}, f32[2,2,256,256]{3,2,1,0:T(8,128)}, u32[]{:S(2)}) copy-start(f32[2,2,256,256]{3,2,1,0:T(8,128)} %probe.1) | copy-start | bytes 3145732
  54.0 2.3 %collective-permute-start.4 = (f32[5,128,256]{2,1,0:T(8,128)S(1)}, f32[5,128,256]{2,1,0:T(8,128)}, u32[]{:S(2)}, u32[]{:S(2)}) collective-permute-start(f32[5,128,256]{2,1,0:T(8,128)S(1)} %constant_dynamic-slice_fusion.2), channel_id=1, source_target_pairs={{0,8},{8,0},{16,24},{24,16},{1,9},{9,1},{17,25},{25,17},{2,10},{10... | collective-permute-start | bytes 1966088 | tf_op jit(solution)/shard_map/ppermute | solution.py:539
  58.3 5.2 %collective-permute-start.6 = (s32[1,17]{1,0:T(1,128)S(1)}, s32[1,17]{1,0:T(1,128)S(1)}, u32[]{:S(2)}, u32[]{:S(2)}) collective-permute-start(s32[1,17]{1,0:T(1,128)S(1)} %pad_add_fusion.3), channel_id=1, source_target_pairs={{0,1},{1,2},{2,3},{3,4},{4,5},{5,6},{6,7},{8,9},{9,10},{10,11},{11... | collective-permute-start | bytes 212 | tf_op jit(solution)/shard_map/ppermute | solution.py:534
  63.5 5.8 %collective-permute-start.7 = (s32[2,17]{1,0:T(2,128)S(1)}, s32[2,17]{1,0:T(2,128)S(1)}, u32[]{:S(2)}, u32[]{:S(2)}) collective-permute-start(s32[2,17]{1,0:T(2,128)S(1)} %pad_add_fusion.2), channel_id=1, source_target_pairs={{0,8},{8,16},{16,24},{1,9},{9,17},{17,25},{2,10},{10,18},{18,26},{... | collective-permute-start | bytes 416 | tf_op jit(solution)/shard_map/ppermute | solution.py:534
  68.6 8.6 %collective-permute-start.5 = (f32[5,64,256]{2,1,0:T(8,128)}, f32[5,64,256]{2,1,0:T(8,128)S(1)}, u32[]{:S(2)}, u32[]{:S(2)}) collective-permute-start(f32[5,64,256]{2,1,0:T(8,128)} %get-tuple-element.56), channel_id=1, source_target_pairs={{0,16},{8,24},{16,0},{24,8},{1,17},{9,25},{17,1},{25,9},{2,18},{10... | collective-permute-start | bytes 983048 | tf_op jit(solution)/shard_map/ppermute | solution.py:539
  69.5 23.7 %copy-start.9 = (f32[2,512,256]{2,1,0:T(8,128)S(1)}, f32[2,512,256]{2,1,0:T(8,128)}, u32[]{:S(2)}) copy-start(f32[2,512,256]{2,1,0:T(8,128)} %copy-done.8) | copy-start | bytes 3145732
  69.5 26.8 %copy-start.7 = (f32[2,256,512]{2,1,0:T(8,128)S(1)}, f32[2,256,512]{2,1,0:T(8,128)}, u32[]{:S(2)}) copy-start(f32[2,256,512]{2,1,0:T(8,128)} %copy-done.6) | copy-start | bytes 3145732
  71.7 1.0 copy-start.2
  77.9 24.5 %all-to-all-start = ((f32[8,5,8,256]{3,2,1,0:T(8,128)}), f32[8,5,8,256]{3,2,1,0:T(8,128)S(1)}, u32[]{:S(2)}, u32[]{:S(2)}) async-start(f32[8,5,8,256]{3,2,1,0:T(8,128)} %copy_bitcast_fusion), calls=%async_computation | async-start | bytes 655360 | tf_op jit(solution)/shard_map/all_to_all | solution.py:594
  93.2 36.8 %collective-permute-start.9 = (f32[2,512,256]{2,1,0:T(8,128)S(1)}, f32[2,512,256]{2,1,0:T(8,128)}, u32[]{:S(2)}, u32[]{:S(2)}) collective-permute-start(f32[2,512,256]{2,1,0:T(8,128)S(1)} %copy-done.9), channel_id=1, source_target_pairs={{0,1},{1,2},{2,3},{3,4},{4,5},{5,6},{6,7},{8,9},{9,10},{10,11},{11... | collective-permute-start | bytes 3145736 | tf_op jit(solution)/shard_map/ppermute | solution.py:534
  96.3 33.7 %collective-permute-start.10 = (f32[2,256,512]{2,1,0:T(8,128)S(1)}, f32[2,256,512]{2,1,0:T(8,128)}, u32[]{:S(2)}, u32[]{:S(2)}) collective-permute-start(f32[2,256,512]{2,1,0:T(8,128)S(1)} %copy-done.7), channel_id=1, source_target_pairs={{0,8},{8,16},{16,24},{1,9},{9,17},{17,25},{2,10},{10,18},{18,26},{... | collective-permute-start | bytes 3145736 | tf_op jit(solution)/shard_map/ppermute | solution.py:534
  100.5 29.4 %collective-permute-start.8 = (f32[2,256,256]{2,1,0:T(8,128)}, f32[2,256,256]{2,1,0:T(8,128)}, u32[]{:S(2)}, u32[]{:S(2)}) collective-permute-start(f32[2,256,256]{2,1,0:T(8,128)} %copy-done.12), channel_id=1, source_target_pairs={{0,8},{8,16},{16,24},{1,9},{9,17},{17,25},{2,10},{10,18},{18,26},{... | collective-permute-start | bytes 1572872 | tf_op jit(solution)/shard_map/ppermute | solution.py:534
  129.9 14.6 %collective-permute-start.12 = (f32[2,256,256]{2,1,0:T(8,128)}, f32[2,256,256]{2,1,0:T(8,128)S(1)}, u32[]{:S(2)}, u32[]{:S(2)}) collective-permute-start(f32[2,256,256]{2,1,0:T(8,128)} %collective-permute-done.8), channel_id=1, source_target_pairs={{0,1},{1,2},{2,3},{3,4},{4,5},{5,6},{6,7},{8,9},{9,10},{10,11},{11... | collective-permute-start | bytes 1572872 | tf_op jit(solution)/shard_map/ppermute | solution.py:534
  131.9 18.6 %collective-permute-start.11 = (f32[4,64,256]{2,1,0:T(8,128)S(1)}, f32[4,64,256]{2,1,0:T(8,128)S(1)}, u32[]{:S(2)}, u32[]{:S(2)}) collective-permute-start(f32[4,64,256]{2,1,0:T(8,128)S(1)} %bitcast.21), channel_id=1, source_target_pairs={{0,16},{8,24},{16,0},{24,8},{1,17},{9,25},{17,1},{25,9},{2,18},{10... | collective-permute-start | bytes 786440 | tf_op jit(solution)/shard_map/ppermute | solution.py:539
  150.5 4.3 %collective-permute-start.13 = (f32[4,128,256]{2,1,0:T(8,128)S(1)}, f32[4,128,256]{2,1,0:T(8,128)S(1)}, u32[]{:S(2)}, u32[]{:S(2)}) collective-permute-start(f32[4,128,256]{2,1,0:T(8,128)S(1)} %pad_maximum_fusion.1), channel_id=1, source_target_pairs={{0,8},{8,0},{16,24},{24,16},{1,9},{9,1},{17,25},{25,17},{2,10},{10... | collective-permute-start | bytes 1572872 | tf_op jit(solution)/shard_map/ppermute | solution.py:539
  (3 other events, 2.6 us)
where the time goes:
time: 157 us; the launch traced here: 156 us
  starting transfers between devices  48.8 us (31%)
  waiting for transfers between devices  38.9 us (25%)
  blocking collectives  27.4 us (17%)
  Pallas kernels  21.2 us (14%)
  local copies, waits for them, and re-layouts  14.5 us (9%)
  other arithmetic  3.56 us (2%)
  between operations  1.72 us (1%)
    ppermute x10, waiting for transfers between devices, from_behind(): return lax.ppermute(array, axis, pairs)  30.8 us
    ppermute x10, starting transfers between devices, from_behind(): return lax.ppermute(array, axis, pairs)  30.2 us
    all_to_all x1, blocking collectives, body(): new = lax.all_to_all(new, 'col', 0, 0, tiled=True)  27.4 us
    all_to_all x1, starting transfers between devices, body(): share = lax.all_to_all(share, 'col', 0, 0, tiled=True).sum(axis=0)  15.2 us
    pallas_call x2, Pallas kernels, visit_slots(): pl.pallas_call(kernel, out_shape=[jax.ShapeDtypeStruct(shape, F32) for sh...  12.1 us
    unnamed x41, local copies, waits for them, and re-layouts  9.8 us
    ppermute x4, waiting for transfers between devices, exchange(): return lax.ppermute(array, axis, [(i, i ^ bit) for i in range(count)])  8.1 us
    pallas_call x1, Pallas kernels, finish(): pl.pallas_call(finish_kernel, grid=(rows // block,), out_shape=jax.ShapeD...  5.09 us
  transfers between devices with their start and end apart: 15, of which 8 were waited for; matrix products, arithmetic and copies ran while one was open for 1% of the time, Pallas kernels for 7%

commit v1 on v0

--- a/solution.py
+++ b/solution.py
@@ -155,14 +155,14 @@
             pltpu.VMEM((size + 16, size), F32),
             pltpu.VMEM((tile_shape[0] + 2 * size, tile_shape[1] + 2 * size), F32),
         ],
-        compiler_params=pltpu.CompilerParams(vmem_limit_bytes=16 * MIB),
+        compiler_params=pltpu.CompilerParams(vmem_limit_bytes=8 * MIB),
         cost_estimate=pl.CostEstimate(flops=4_000_000_000, bytes_accessed=16_000_000, transcendentals=0),
         name="light",
     )(meta, probe)
 
 
 def arrange_kernel(meta, amplitudes, order_rows, order_cols, out):
-    @pl.loop(0, meta[0, meta.shape[1] - 1])
+    @pl.loop(0, meta[0, 2 * amplitudes.shape[0]])
     def _(slot):
         x = dot(order_rows[...], jnp.concatenate(split_three(amplitudes[slot]), axis=0))
         out[slot] = dot(jnp.concatenate(split_three(x), axis=1), order_cols[...])
@@ -176,7 +176,7 @@
         out_shape=jax.ShapeDtypeStruct(amplitudes.shape, F32),
         in_specs=[pl.BlockSpec(memory_space=pltpu.SMEM)] + [vmem] * 3,
         out_specs=vmem,
-        compiler_params=pltpu.CompilerParams(vmem_limit_bytes=16 * MIB),
+        compiler_params=pltpu.CompilerParams(vmem_limit_bytes=8 * MIB),
         cost_estimate=pl.CostEstimate(flops=2_000_000_000, bytes_accessed=8_000_000, transcendentals=0),
         name="arrange",
     )(meta, amplitudes, order_rows, order_cols)
@@ -202,7 +202,7 @@
 
 def slots_kernel(
     needs_rim, meta, probe, amplitudes, sources, forward_t, backward_t, init, outs, probe_out,
-    ext, grid, amp, chosen, patch_f, patch_b, x_f, y_f, z_f, g_s, x_b, z_b, back, template, sems,
+    ext, grid, chosen, patch_f, patch_b, x_f, y_f, z_f, g_s, x_b, z_b, back, template, sems,
 ):
     size = probe.shape[2]
     half = size // 2
@@ -210,7 +210,7 @@
     slots = amplitudes.shape[0]
     tile_rows, tile_cols = (n - size for n in ext.shape[1:])
     step = 32
-    load_sems, amp_sems, out_sems = sems
+    load_sems, out_sems = sems
 
     regions = (
         (pl.ds(0, tile_rows), pl.ds(0, tile_cols)),
@@ -229,9 +229,6 @@
     for load in loads:
         load.start()
 
-    def amp_copy(slot):
-        return pltpu.make_async_copy(amplitudes.at[slot], amp.at[slot], amp_sems.at[slot])
-
     def choose(slot, found):
         beyond = meta[0, 2 * slot + 1] + size > tile_cols
         wanted = beyond if needs_rim else jnp.logical_not(beyond)
@@ -239,7 +236,6 @@
         @pl.when(wanted)
         def _():
             chosen[found] = slot
-            amp_copy(slot).start()
 
         return found + wanted.astype(jnp.int32)
 
@@ -316,13 +312,11 @@
             )
 
         def scale(v, at):
-            if v == 0 and at == 0:
-                amp_copy(slot).wait()
             waves = [z_f[v, pl.ds(m * size + at, step), :] for m in range(modes)]
             total = jnp.zeros((step, half), F32)
             for wave in waves:
                 total += wave[:, :half] * wave[:, :half] + wave[:, half:] * wave[:, half:]
-            measured = amp[slot, pl.ds(at, step), pl.ds(v * half, half)]
+            measured = amplitudes[slot, pl.ds(at, step), pl.ds(v * half, half)]
             factor = measured * lax.rsqrt(jnp.maximum(total, FLOOR * FLOOR)) - 1.0
             factor = jnp.concatenate([factor, factor], axis=1)
             for m in range(modes):
@@ -422,9 +416,9 @@
     if needs_rim:
         parts = [
             grid.at[:, pl.ds(0, tile_rows), pl.ds(0, tile_cols)],
-            grid.at[:, pl.ds(0, tile_rows), pl.ds(tile_cols, size)],
+            grid.at[:, :, pl.ds(tile_cols, size)],
             grid.at[:, pl.ds(tile_rows, size), pl.ds(0, tile_cols)],
-            grid.at[:, pl.ds(tile_rows, size), pl.ds(tile_cols, size)],
+            probe_out.at[:, pl.ds(pl.multiple_of(meta[0, 2 * slots + 1] * half, half), half)],
         ]
     else:
         parts = [grid.at[:, :, pl.ds(0, tile_cols)]]
@@ -445,7 +439,7 @@
     anywhere = pl.BlockSpec(memory_space=pl.ANY)
     needs_rim = bool(init)
     if needs_rim:
-        shapes = [(2, rows, cols), (2, rows, size), (2, size, cols), (2, size, size)]
+        shapes = [(2, rows, cols), (2, rows + size, size), (2, size, cols), (2 * modes + 1, size // 2, size)]
     else:
         shapes = [(2, rows + size, cols)]
     splits = np.cumsum([1, 1, 1, len(sources), 1, 1, len(init), len(shapes), 1])
@@ -457,20 +451,19 @@
         scratch = refs[splits[-1] :]
         slots_kernel(
             needs_rim, meta[0], probe[0], amplitudes[0], sources, forward_t[0], backward_t[0], init, outs,
-            probe_out[0], *scratch[:-3], scratch[-3:],
+            probe_out[0], *scratch[:-2], scratch[-2:],
         )
 
     return pl.pallas_call(
         kernel,
         out_shape=[jax.ShapeDtypeStruct(shape, F32) for shape in shapes]
         + [jax.ShapeDtypeStruct((2 * modes + 1, size, size), F32)],
-        in_specs=[pl.BlockSpec(memory_space=pltpu.SMEM), vmem] + [anywhere] * (1 + len(sources))
+        in_specs=[pl.BlockSpec(memory_space=pltpu.SMEM), vmem, vmem] + [anywhere] * len(sources)
         + [vmem] * 2 + [anywhere] * len(init),
         out_specs=[anywhere] * len(shapes) + [vmem],
         scratch_shapes=[
             pltpu.VMEM((2, rows + size, cols + size), F32),
             pltpu.VMEM((2, rows + size, cols + size), F32),
-            pltpu.VMEM(amplitudes.shape, F32),
             pltpu.SMEM((slots,), jnp.int32),
             pltpu.VMEM((2, size, size), F32),
             pltpu.VMEM((2, size, size), F32),
@@ -483,10 +476,9 @@
             pltpu.VMEM((modes, 2, size, size), F32),
             pltpu.VMEM((2, size + 16, size), F32),
             pltpu.SemaphoreType.DMA((7,)),
-            pltpu.SemaphoreType.DMA((slots,)),
             pltpu.SemaphoreType.DMA((4,)),
         ],
-        compiler_params=pltpu.CompilerParams(vmem_limit_bytes=32 * MIB),
+        compiler_params=pltpu.CompilerParams(vmem_limit_bytes=28 * MIB),
         cost_estimate=pl.CostEstimate(flops=12_000_000_000, bytes_accessed=16_000_000, transcendentals=0),
         name="slots_beyond" if needs_rim else "slots_inside",
     )(meta, probe, amplitudes, *sources, *tables, *init)
@@ -523,6 +515,7 @@
             whole,
         ],
         out_specs=whole,
+        compiler_params=pltpu.CompilerParams(vmem_limit_bytes=8 * MIB),
         cost_estimate=pl.CostEstimate(flops=3_000_000, bytes_accessed=12_000_000, transcendentals=0),
         name="finish",
     )(own, right, lower, corner, inverse_light, tile)
@@ -541,6 +534,60 @@
 
 def together(*arrays):
     return lax.optimization_barrier(arrays)
+
+
+def cut(tile, size):
+    rows, cols = tile.shape[1:]
+    regions = ((0, size, size), (0, size, cols), (size, rows - size, size))
+
+    def kernel(tile, *refs):
+        sems = refs[-1]
+        copies = [
+            pltpu.make_async_copy(tile.at[:, pl.ds(at, height), pl.ds(0, width)], out, sems.at[i])
+            for i, ((at, height, width), out) in enumerate(zip(regions, refs[:-1]))
+        ]
+        for copy in copies:
+            copy.start()
+        for copy in copies:
+            copy.wait()
+
+    anywhere = pl.BlockSpec(memory_space=pl.ANY)
+    return pl.pallas_call(
+        kernel,
+        out_shape=[jax.ShapeDtypeStruct((2, height, width), F32) for _, height, width in regions],
+        in_specs=[anywhere],
+        out_specs=[anywhere] * len(regions),
+        scratch_shapes=[pltpu.SemaphoreType.DMA((len(regions),))],
+        compiler_params=pltpu.CompilerParams(vmem_limit_bytes=MIB),
+        cost_estimate=pl.CostEstimate(flops=0, bytes_accessed=4_000_000, transcendentals=0),
+        name="cut",
+    )(tile)
+
+
+def join(upper, mine, other):
+    half = mine.shape[1]
+
+    def kernel(upper, mine, other, out, sems):
+        copies = [
+            pltpu.make_async_copy(source, out.at[:, pl.ds(pl.multiple_of(at * half, half), half)], sems.at[i])
+            for i, (source, at) in enumerate(((mine, upper[0]), (other, 1 - upper[0])))
+        ]
+        for copy in copies:
+            copy.start()
+        for copy in copies:
+            copy.wait()
+
+    anywhere = pl.BlockSpec(memory_space=pl.ANY)
+    return pl.pallas_call(
+        kernel,
+        out_shape=jax.ShapeDtypeStruct((mine.shape[0], 2 * half) + mine.shape[2:], F32),
+        in_specs=[pl.BlockSpec(memory_space=pltpu.SMEM), anywhere, anywhere],
+        out_specs=anywhere,
+        scratch_shapes=[pltpu.SemaphoreType.DMA((2,))],
+        compiler_params=pltpu.CompilerParams(vmem_limit_bytes=MIB),
+        cost_estimate=pl.CostEstimate(flops=0, bytes_accessed=2_000_000, transcendentals=0),
+        name="join",
+    )(upper.reshape(1), mine, other)
 
 
 def body(object_field, probe, amplitudes, positions, counts):
@@ -548,48 +595,51 @@
     tile_rows, tile_cols = object_field.shape[1:]
     slots = amplitudes.shape[0]
     origin = jnp.stack([lax.axis_index("row") * tile_rows, lax.axis_index("col") * tile_cols]).astype(jnp.int32)
+    bits = [1 << k for k in range(lax.axis_size("row").bit_length() - 1)]
+    uppers = [(lax.axis_index("row") & bit) // bit for bit in bits]
 
     def relative(table):
         return jnp.concatenate([table[:, : 2 * slots] - jnp.tile(origin, slots)[None], table[:, 2 * slots :]], axis=1)
 
+    right_up, lower, rest = cut(object_field, size)
+    right_up = from_behind(right_up, "col", -1)
+    lower = from_behind(lower, "row", -1)
+
     meta = jnp.concatenate([positions.reshape(1, 2 * slots), counts.reshape(1, 1)], axis=1)
-    mine = relative(meta)
-
-    right_up = from_behind(object_field[:, :size, :size], "col", -1)
-    lower = from_behind(object_field[:, :size, :], "row", -1)
+    mine = jnp.concatenate([relative(meta), (1 - uppers[0]).astype(jnp.int32).reshape(1, 1)], axis=1)
     amplitudes = arrange(mine, amplitudes)
-    right_up, amplitudes, rest = together(right_up, amplitudes, object_field[:, size:, :size])
+    amplitudes, rest = together(amplitudes, rest)
+    right_down = from_behind(rest, "col", -1)
+    table = jnp.concatenate([meta, from_behind(meta, "col", 1)], axis=0)
+    table = relative(jnp.concatenate([table, from_behind(table, "row", 1)], axis=0))
+    right_up, amplitudes, lower, table = together(right_up, amplitudes, lower, table)
     corner = from_behind(right_up, "row", -1)
-    right_down = from_behind(rest, "col", -1)
     init = visit_slots(mine, probe, amplitudes, [object_field, lower], [])
     right_up, right_down, corner, *init = together(right_up, right_down, corner, *init)
-    own, right_spill, lower_spill, corner_spill, sums = visit_slots(
+    own, right_spill, lower_spill, send, share = visit_slots(
         mine, probe, amplitudes, [object_field, lower, right_up, right_down, corner], list(init)
     )
-    corner_spill = from_behind(corner_spill, "row", 1)
-    right_spill = from_behind(right_spill, "col", 1)
-    lower_spill = from_behind(lower_spill, "row", 1)
-
-    share = sums
+
     start = jnp.zeros((), jnp.int32)
-    bits = [1 << k for k in range(lax.axis_size("row").bit_length() - 1)]
-    inverse_light = None
-    for bit in bits:
+    got = None
+    for bit, upper in zip(bits, uppers):
         half = share.shape[1] // 2
-        upper = (lax.axis_index("row") // bit) % 2
-        keep = lax.dynamic_slice_in_dim(share, upper * half, half, axis=1)
-        send = lax.dynamic_slice_in_dim(share, (1 - upper) * half, half, axis=1)
+        if got is not None:
+            send = lax.dynamic_slice_in_dim(share, (1 - upper) * half, half, axis=1)
         got = exchange(send, "row", bit)
+        if bit == bits[0]:
+            right_spill = from_behind(right_spill, "col", 1)
+            lower_spill = from_behind(lower_spill, "row", 1)
         if bit == bits[-1]:
-            meta, keep = together(meta, keep)
-            table = jnp.concatenate([meta, from_behind(meta, "col", 1)], axis=0)
-            table = jnp.concatenate([table, from_behind(table, "row", 1)], axis=0)
-            inverse_light = light(relative(table), probe, (tile_rows, tile_cols))
+            table, send = together(table, send)
+            inverse_light = light(table, probe, (tile_rows, tile_cols))
             got, inverse_light = together(got, inverse_light)
-        share = keep + got
+        share = lax.dynamic_slice_in_dim(share, upper * half, half, axis=1) + got
         start = start + upper * half
     parts = lax.axis_size("col")
     rows = share.shape[1] // parts
+    share, right_spill, lower_spill = together(share, right_spill, lower_spill)
+    corner_spill = from_behind(right_spill[:, tile_rows:], "row", 1)
     share = share.reshape(2 * modes + 1, parts, rows, size).transpose(1, 0, 2, 3)
     share = lax.all_to_all(share, "col", 0, 0, tiled=True).sum(axis=0)
     old = lax.dynamic_slice_in_dim(
@@ -599,15 +649,13 @@
     new = jnp.broadcast_to(new[None], (parts,) + new.shape)
     new = lax.all_to_all(new, "col", 0, 0, tiled=True)
     new = new.transpose(1, 0, 2, 3).reshape(2 * modes, parts * rows, size)
-    new, corner_spill, right_spill, lower_spill = together(new, corner_spill, right_spill, lower_spill)
-    corner_spill = from_behind(corner_spill, "col", 1)
-    for bit in reversed(bits):
-        upper = (lax.axis_index("row") // bit) % 2 == 1
+    new, corner_spill = together(new, corner_spill)
+    for bit, upper in reversed(list(zip(bits, uppers))):
         other = exchange(new, "row", bit)
         if bit == bits[-1]:
             new_object = finish(own, right_spill, lower_spill, corner_spill, inverse_light, object_field)
             other, new_object = together(other, new_object)
-        new = jnp.concatenate([jnp.where(upper, other, new), jnp.where(upper, new, other)], axis=1)
+        new = join(upper, new, other)
     return (new_object, new.reshape(modes, 2, size, size))
 
 

time: 157 us -> 153 us (0.975)
  the two profiles are of different devices: /device:TPU:17 before, /device:TPU:0 now
where the time goes in v1:
time: 153 us
  starting transfers between devices  57.5 us (38%)
  waiting for transfers between devices  44.2 us (29%)
  Pallas kernels  27.4 us (18%)
  local copies, waits for them, and re-layouts  19.1 us (12%)
  other arithmetic  3.3 us (2%)
  between operations  1.77 us (1%)
    ppermute x4, starting transfers between devices, exchange(): return lax.ppermute(array, axis, [(i, i ^ bit) for i in range(count)])  27.9 us
    ppermute x9, waiting for transfers between devices, from_behind(): return lax.ppermute(array, axis, pairs)  22.7 us
    ppermute x9, starting transfers between devices, from_behind(): return lax.ppermute(array, axis, pairs)  20.2 us
    pallas_call x2, Pallas kernels, visit_slots(): pl.pallas_call(kernel, out_shape=[jax.ShapeDtypeStruct(shape, F32) for sh...  16.9 us
    unnamed x39, local copies, waits for them, and re-layouts  15.4 us
    all_to_all x1, waiting for transfers between devices, body(): share = lax.all_to_all(share, 'col', 0, 0, tiled=True).sum(axis=0)  9.59 us
    ppermute x4, waiting for transfers between devices, exchange(): return lax.ppermute(array, axis, [(i, i ^ bit) for i in range(count)])  7.39 us
    all_to_all x1, starting transfers between devices, body(): share = lax.all_to_all(share, 'col', 0, 0, tiled=True).sum(axis=0)  5.76 us
  transfers between devices with their start and end apart: 15, of which 6 were waited for; matrix products, arithmetic and copies ran while one was open for 3% of the time, Pallas kernels for 11%

profile of v1, /device:TPU:0, one launch (start us, length us, event | category | flops | bytes accessed | tf_op | source)
XLA Modules:
  0.0 153.3 jit_solution(15646238204537187055)
XLA Ops:
  0.6 1.6 %copy-done = f32[2,512,512]{2,1,0:T(8,128)S(1)} copy-done((f32[2,512,512]{2,1,0:T(8,128)S(1)}, f32[2,512,512]{2,1,0:T(8,128)}, u32[]{:S(2)}) %copy-start) | copy-done | bytes 2097176
  2.2 1.4 cut.1
  3.6 1.3 collective-permute-start.1
  6.3 4.9 %collective-permute-start.2 = (s32[1,17]{1,0:T(1,128)}, s32[1,17]{1,0:T(1,128)S(1)}, u32[]{:S(2)}, u32[]{:S(2)}) collective-permute-start(s32[1,17]{1,0:T(1,128)} %pad_add_fusion.5), channel_id=1, source_target_pairs={{0,1},{1,2},{2,3},{3,4},{4,5},{5,6},{6,7},{8,9},{9,10},{10,11},{11... | collective-permute-start | bytes 212 | tf_op jit(solution)/shard_map/ppermute | solution.py:527
  11.2 1.3 collective-permute-start
  12.7 1.6 %copy-done.9 = f32[8,256,256]{2,1,0:T(8,128)S(1)} copy-done((f32[8,256,256]{2,1,0:T(8,128)S(1)}, f32[8,256,256]{2,1,0:T(8,128)}, u32[]{:S(2)}) %copy-start.9) | copy-done | bytes 2097176
  15.3 2.4 %arrange.1.refs_2_ = f32[8,256,256]{2,1,0:T(8,128)S(1)} custom-call(s32[1,18]{1,0:T(1,128)S(1)} %pad_add_fusion.4.meta.refs_0_, f32[8,256,256]{2,1,0:T(8,128)S(1)} %copy-done.9, bf16[256,768]{1,0:T(8,128)(2,1)S(1)} %copy-done.14, bf16[768,256]{1,0:T(8,128)(2,1)S(1)} %copy-done.15), custom_call_target="tpu_custom_call" | custom-call | flops 2000000000 | bytes 8000000 | tf_op jit(solution)/shard_map/arrange/pallas_call | solution.py:174
  17.7 1.3 copy-done.16
  19.1 3.4 %collective-permute-start.3 = (s32[2,17]{1,0:T(2,128)S(1)}, s32[2,17]{1,0:T(2,128)S(1)}, u32[]{:S(2)}, u32[]{:S(2)}) collective-permute-start(s32[2,17]{1,0:T(2,128)S(1)} %pad_add_fusion.2), channel_id=1, source_target_pairs={{0,8},{8,16},{16,24},{1,9},{9,17},{17,25},{2,10},{10,18},{18,26},{... | collective-permute-start | bytes 416 | tf_op jit(solution)/shard_map/ppermute | solution.py:527
  24.1 4.0 %collective-permute-done.refs_5_ = f32[2,256,256]{2,1,0:T(8,128)} collective-permute-done((f32[2,256,256]{2,1,0:T(8,128)}, f32[2,256,256]{2,1,0:T(8,128)}, u32[]{:S(2)}, u32[]{:S(2)}) %collective-permute-start) | collective-permute-done | bytes 524320 | tf_op jit(solution)/shard_map/ppermute | solution.py:527
  31.5 1.6 %copy-done.17 = f32[8,256,256]{2,1,0:T(8,128)S(1)} copy-done((f32[8,256,256]{2,1,0:T(8,128)S(1)}, f32[8,256,256]{2,1,0:T(8,128)}, u32[]{:S(2)}) %copy-start.17) | copy-done | bytes 2097176
  33.1 8.9 %slots_inside.1 = (f32[2,768,512]{2,1,0:T(8,128)S(1)}, f32[5,256,256]{2,1,0:T(8,128)S(1)}) custom-call(s32[1,18]{1,0:T(1,128)S(1)} %pad_add_fusion.4.meta.refs_0_, f32[2,2,256,256]{3,2,1,0:T(8,128)S(1)} %copy-done.7, f32[8,256,256]{2,1,0:T(8,128)S(1)} %copy-done.17, f32[2,512,512]{2,1,0:T(8,128)S(1)} %copy-done.1, ...), custom_call_target="tpu_custom_call" | custom-call | flops 12000000000 | bytes 16000000 | tf_op jit(solution)/shard_map/slots_inside/pallas_call | solution.py:457
  42.0 8.0 %slots_beyond.1 = (f32[2,512,512]{2,1,0:T(8,128)S(1)}, f32[2,768,256]{2,1,0:T(8,128)}, f32[2,256,512]{2,1,0:T(8,128)}, f32[5,128,256]{2,1,0:T(8,128)}, f32[5,256,256]{2,1,0:T(8,128)S(1)}) custom-call(s32[1,18]{1,0:T(1,128)S(1)} %pad_add_fusion.4.meta.refs_0_, f32[2,2,256,256]{3,2,1,0:T(8,128)S(1)} %copy-done.7, f32[8,256,256]{2,1,0:T(8,128)S(1)} %copy-done.17, ...), custom_call_target="tpu_custom_call" | custom-call | flops 12000000000 | bytes 16000000 | tf_op jit(solution)/shard_map/slots_beyond/pallas_call | solution.py:457
  50.0 1.3 copy-done.2
  52.4 5.9 %collective-permute-start.6 = (f32[5,128,256]{2,1,0:T(8,128)}, f32[5,128,256]{2,1,0:T(8,128)}, u32[]{:S(2)}, u32[]{:S(2)}) collective-permute-start(f32[5,128,256]{2,1,0:T(8,128)} %get-tuple-element.49), channel_id=1, source_target_pairs={{0,8},{8,0},{16,24},{24,16},{1,9},{9,1},{17,25},{25,17},{2,10},{10... | collective-permute-start | bytes 1966088 | tf_op jit(solution)/shard_map/ppermute | solution.py:532
  58.3 3.1 %collective-permute-start.8 = (f32[2,768,256]{2,1,0:T(8,128)}, f32[2,768,256]{2,1,0:T(8,128)}, u32[]{:S(2)}, u32[]{:S(2)}) collective-permute-start(f32[2,768,256]{2,1,0:T(8,128)} %get-tuple-element.53), channel_id=1, source_target_pairs={{0,1},{1,2},{2,3},{3,4},{4,5},{5,6},{6,7},{8,9},{9,10},{10,11},{11... | collective-permute-start | bytes 4718600 | tf_op jit(solution)/shard_map/ppermute | solution.py:527
  61.4 1.7 %collective-permute-start.9 = (f32[2,256,512]{2,1,0:T(8,128)}, f32[2,256,512]{2,1,0:T(8,128)S(1)}, u32[]{:S(2)}, u32[]{:S(2)}) collective-permute-start(f32[2,256,512]{2,1,0:T(8,128)} %get-tuple-element.54), channel_id=1, source_target_pairs={{0,8},{8,16},{16,24},{1,9},{9,17},{17,25},{2,10},{10,18},{18,26},{... | collective-permute-start | bytes 3145736 | tf_op jit(solution)/shard_map/ppermute | solution.py:527
  63.1 1.5 dynamic-slice_add_fusion
  64.6 2.8 %collective-permute-start.7 = (f32[5,64,256]{2,1,0:T(8,128)S(1)}, f32[5,64,256]{2,1,0:T(8,128)S(1)}, u32[]{:S(2)}, u32[]{:S(2)}) collective-permute-start(f32[5,64,256]{2,1,0:T(8,128)S(1)} %constant_dynamic-slice_fusion), channel_id=1, source_target_pairs={{0,16},{8,24},{16,0},{24,8},{1,17},{9,25},{17,1},{25,9},{2,18},{10... | collective-permute-start | bytes 983048 | tf_op jit(solution)/shard_map/ppermute | solution.py:532
  67.4 1.7 %light.1.inverse_light = f32[512,512]{1,0:T(8,128)S(1)} custom-call(s32[4,17]{1,0:T(4,128)S(1)} %pad_add_fusion.1.meta, f32[2,2,256,256]{3,2,1,0:T(8,128)S(1)} %copy-done.8), custom_call_target="tpu_custom_call" | custom-call | flops 4000000000 | bytes 16000000 | tf_op jit(solution)/shard_map/light/pallas_call | solution.py:149
  70.1 5.5 %collective-permute-done.7 = f32[5,64,256]{2,1,0:T(8,128)S(1)} collective-permute-done((f32[5,64,256]{2,1,0:T(8,128)S(1)}, f32[5,64,256]{2,1,0:T(8,128)S(1)}, u32[]{:S(2)}, u32[]{:S(2)}) %collective-permute-start.7) | collective-permute-done | bytes 327712 | tf_op jit(solution)/shard_map/ppermute | solution.py:532
  75.7 18.7 %collective-permute-done.8.right = f32[2,768,256]{2,1,0:T(8,128)} collective-permute-done((f32[2,768,256]{2,1,0:T(8,128)}, f32[2,768,256]{2,1,0:T(8,128)}, u32[]{:S(2)}, u32[]{:S(2)}) %collective-permute-start.8) | collective-permute-done | bytes 1572896 | tf_op jit(solution)/shard_map/ppermute | solution.py:527
  95.1 5.8 %all-to-all-start = ((f32[8,5,8,256]{3,2,1,0:T(8,128)}), f32[8,5,8,256]{3,2,1,0:T(8,128)S(1)}, u32[]{:S(2)}, u32[]{:S(2)}) async-start(f32[8,5,8,256]{3,2,1,0:T(8,128)} %copy_bitcast_fusion), calls=%async_computation | async-start | bytes 655360 | tf_op jit(solution)/shard_map/all_to_all | solution.py:644
  100.9 9.6 %all-to-all-done = f32[8,5,8,256]{3,2,1,0:T(8,128)S(1)} async-done(((f32[8,5,8,256]{3,2,1,0:T(8,128)}), f32[8,5,8,256]{3,2,1,0:T(8,128)S(1)}, u32[]{:S(2)}, u32[]{:S(2)}) %all-to-all-start) | async-done | bytes 327712 | tf_op jit(solution)/shard_map/all_to_all | solution.py:644
  112.0 3.6 %all-to-all-start.1 = ((f32[8,4,8,256]{3,2,1,0:T(8,128)}), f32[8,4,8,256]{3,2,1,0:T(8,128)S(1)}, u32[]{:S(2)}, u32[]{:S(2)}) async-start(f32[8,4,8,256]{3,2,1,0:T(8,128)} %broadcast_in_dim.2), calls=%async_computation.1 | async-start | bytes 524288 | tf_op jit(solution)/shard_map/all_to_all | solution.py:650
  115.6 1.9 %slice.19 = f32[2,256,256]{2,1,0:T(8,128)} slice(f32[2,768,256]{2,1,0:T(8,128)} %collective-permute-done.8.right), slice={[0:2], [512:768], [0:256]} | slice | bytes 1048576 | tf_op jit(solution)/shard_map/slice | solution.py:642
  117.5 2.1 %collective-permute-start.10 = (f32[2,256,256]{2,1,0:T(8,128)}, f32[2,256,256]{2,1,0:T(8,128)}, u32[]{:S(2)}, u32[]{:S(2)}) collective-permute-start(f32[2,256,256]{2,1,0:T(8,128)} %slice.19), channel_id=1, source_target_pairs={{0,8},{8,16},{16,24},{1,9},{9,17},{17,25},{2,10},{10,18},{18,26},{... | collective-permute-start | bytes 1572872 | tf_op jit(solution)/shard_map/ppermute | solution.py:527
  119.6 4.5 %all-to-all-done.1 = f32[8,4,8,256]{3,2,1,0:T(8,128)S(1)} async-done(((f32[8,4,8,256]{3,2,1,0:T(8,128)}), f32[8,4,8,256]{3,2,1,0:T(8,128)S(1)}, u32[]{:S(2)}, u32[]{:S(2)}) %all-to-all-start.1) | async-done | bytes 262176 | tf_op jit(solution)/shard_map/all_to_all | solution.py:650
  124.2 19.1 %collective-permute-start.11 = (f32[4,64,256]{2,1,0:T(8,128)S(1)}, f32[4,64,256]{2,1,0:T(8,128)S(1)}, u32[]{:S(2)}, u32[]{:S(2)}) collective-permute-start(f32[4,64,256]{2,1,0:T(8,128)S(1)} %copy_bitcast_fusion.1.mine), channel_id=1, source_target_pairs={{0,16},{8,24},{16,0},{24,8},{1,17},{9,25},{17,1},{25,9},{2,18},{10... | collective-permute-start | bytes 786440 | tf_op jit(solution)/shard_map/ppermute | solution.py:532
  143.2 1.6 %copy-done.3 = f32[2,512,512]{2,1,0:T(8,128)S(1)} copy-done((f32[2,512,512]{2,1,0:T(8,128)S(1)}, f32[2,512,512]{2,1,0:T(8,128)}, u32[]{:S(2)}) %copy-start.3) | copy-done | bytes 2097176
  146.0 4.0 %finish.1 = f32[2,512,512]{2,1,0:T(8,128)} custom-call(f32[2,512,512]{2,1,0:T(8,128)S(1)} %copy-done.3, f32[2,768,256]{2,1,0:T(8,128)} %collective-permute-done.8.right, f32[2,256,512]{2,1,0:T(8,128)S(1)} %collective-permute-done.9.lower, f32[2,256,256]{2,1,0:T(8,128)} %collective-permute-done.10.corner, f32[512,512]{1,0:T(8,128)S(1)} %copy-done.5, ...), custom_call_target="tpu_custom_call" | custom-call | flops 3000000 | bytes 12000000 | tf_op jit(solution)/shard_map/finish/pallas_call | solution.py:505
  150.2 1.9 %collective-permute-done.12.other = f32[4,128,256]{2,1,0:T(8,128)S(1)} collective-permute-done((f32[4,128,256]{2,1,0:T(8,128)S(1)}, f32[4,128,256]{2,1,0:T(8,128)S(1)}, u32[]{:S(2)}, u32[]{:S(2)}) %collective-permute-start.12) | collective-permute-done | bytes 524320 | tf_op jit(solution)/shard_map/ppermute | solution.py:532
  (68 shorter events, 13.8 us)
Async XLA Ops:
  0.6 1.6 %copy-start = (f32[2,512,512]{2,1,0:T(8,128)S(1)}, f32[2,512,512]{2,1,0:T(8,128)}, u32[]{:S(2)}) copy-start(f32[2,512,512]{2,1,0:T(8,128)} %tile.6) | copy-start | bytes 6291460
  2.2 2.7 %copy-start.18 = (s32[8,2]{0,1:T(2,128)S(1)}, s32[8,2]{0,1:T(2,128)}, u32[]{:S(2)}) copy-start(s32[8,2]{0,1:T(2,128)} %param.14) | copy-start | bytes 196
  2.2 10.5 %copy-start.14 = (bf16[256,768]{1,0:T(8,128)(2,1)S(1)}, bf16[256,768]{1,0:T(8,128)(2,1)}, u32[]{:S(2)}) copy-start(bf16[256,768]{1,0:T(8,128)(2,1)} %constant.55.clone.order_rows) | copy-start | bytes 1179652
  3.6 24.5 %collective-permute-start.1 = (f32[2,256,512]{2,1,0:T(8,128)}, f32[2,256,512]{2,1,0:T(8,128)}, u32[]{:S(2)}, u32[]{:S(2)}) collective-permute-start(f32[2,256,512]{2,1,0:T(8,128)} %get-tuple-element.36), channel_id=1, source_target_pairs={{8,0},{16,8},{24,16},{9,1},{17,9},{25,17},{10,2},{18,10},{26,18},{... | collective-permute-start | bytes 3145736 | tf_op jit(solution)/shard_map/ppermute | solution.py:527
  6.3 12.7 %collective-permute-start.2 = (s32[1,17]{1,0:T(1,128)}, s32[1,17]{1,0:T(1,128)S(1)}, u32[]{:S(2)}, u32[]{:S(2)}) collective-permute-start(s32[1,17]{1,0:T(1,128)} %pad_add_fusion.5), channel_id=1, source_target_pairs={{0,1},{1,2},{2,3},{3,4},{4,5},{5,6},{6,7},{8,9},{9,10},{10,11},{11... | collective-permute-start | bytes 212 | tf_op jit(solution)/shard_map/ppermute | solution.py:527
  11.2 16.9 %collective-permute-start = (f32[2,256,256]{2,1,0:T(8,128)}, f32[2,256,256]{2,1,0:T(8,128)}, u32[]{:S(2)}, u32[]{:S(2)}) collective-permute-start(f32[2,256,256]{2,1,0:T(8,128)} %get-tuple-element.33), channel_id=1, source_target_pairs={{1,0},{2,1},{3,2},{4,3},{5,4},{6,5},{7,6},{9,8},{10,9},{11,10},{12... | collective-permute-start | bytes 1572872 | tf_op jit(solution)/shard_map/ppermute | solution.py:527
  12.7 1.6 %copy-start.9 = (f32[8,256,256]{2,1,0:T(8,128)S(1)}, f32[8,256,256]{2,1,0:T(8,128)}, u32[]{:S(2)}) copy-start(f32[8,256,256]{2,1,0:T(8,128)} %amplitudes.1) | copy-start | bytes 6291460
  15.3 14.0 %copy-start.1 = (f32[2,512,512]{2,1,0:T(8,128)S(1)}, f32[2,512,512]{2,1,0:T(8,128)}, u32[]{:S(2)}) copy-start(f32[2,512,512]{2,1,0:T(8,128)} %tile.6) | copy-start | bytes 6291460
  15.3 14.0 %copy-start.7 = (f32[2,2,256,256]{3,2,1,0:T(8,128)S(1)}, f32[2,2,256,256]{3,2,1,0:T(8,128)}, u32[]{:S(2)}) copy-start(f32[2,2,256,256]{3,2,1,0:T(8,128)} %probe.1) | copy-start | bytes 3145732
  17.7 1.3 copy-start.16
  19.1 4.7 %collective-permute-start.3 = (s32[2,17]{1,0:T(2,128)S(1)}, s32[2,17]{1,0:T(2,128)S(1)}, u32[]{:S(2)}, u32[]{:S(2)}) collective-permute-start(s32[2,17]{1,0:T(2,128)S(1)} %pad_add_fusion.2), channel_id=1, source_target_pairs={{0,8},{8,16},{16,24},{1,9},{9,17},{17,25},{2,10},{10,18},{18,26},{... | collective-permute-start | bytes 416 | tf_op jit(solution)/shard_map/ppermute | solution.py:527
  22.5 19.4 %collective-permute-start.4 = (f32[2,256,256]{2,1,0:T(8,128)}, f32[2,256,256]{2,1,0:T(8,128)}, u32[]{:S(2)}, u32[]{:S(2)}) collective-permute-start(f32[2,256,256]{2,1,0:T(8,128)} %get-tuple-element.40), channel_id=1, source_target_pairs={{1,0},{2,1},{3,2},{4,3},{5,4},{6,5},{7,6},{9,8},{10,9},{11,10},{12... | collective-permute-start | bytes 1572872 | tf_op jit(solution)/shard_map/ppermute | solution.py:527
  28.1 13.9 %collective-permute-start.5 = (f32[2,256,256]{2,1,0:T(8,128)}, f32[2,256,256]{2,1,0:T(8,128)S(1)}, u32[]{:S(2)}, u32[]{:S(2)}) collective-permute-start(f32[2,256,256]{2,1,0:T(8,128)} %collective-permute-done.refs_5_), channel_id=1, source_target_pairs={{8,0},{16,8},{24,16},{9,1},{17,9},{25,17},{10,2},{18,10},{26,18},{... | collective-permute-start | bytes 1572872 | tf_op jit(solution)/shard_map/ppermute | solution.py:527
  29.4 1.0 copy-start.10
  30.4 1.0 copy-start.12
  31.5 1.6 %copy-start.17 = (f32[8,256,256]{2,1,0:T(8,128)S(1)}, f32[8,256,256]{2,1,0:T(8,128)}, u32[]{:S(2)}) copy-start(f32[8,256,256]{2,1,0:T(8,128)} %copy-done.16) | copy-start | bytes 6291460
  33.1 8.9 %copy-start.11 = (bf16[2,2,256,256]{3,2,1,0:T(8,128)(2,1)S(1)}, bf16[2,2,256,256]{3,2,1,0:T(8,128)(2,1)}, u32[]{:S(2)}) copy-start(bf16[2,2,256,256]{3,2,1,0:T(8,128)(2,1)} %constant.57.clone.refs_5_.refs_8_) | copy-start | bytes 1572868
  33.1 8.9 %copy-start.13 = (bf16[2,2,256,256]{3,2,1,0:T(8,128)(2,1)S(1)}, bf16[2,2,256,256]{3,2,1,0:T(8,128)(2,1)}, u32[]{:S(2)}) copy-start(bf16[2,2,256,256]{3,2,1,0:T(8,128)(2,1)} %constant.58.clone.refs_6_.refs_9_) | copy-start | bytes 1572868
  50.0 1.3 copy-start.2
  51.4 1.1 copy-start.6
  52.4 10.7 %collective-permute-start.6 = (f32[5,128,256]{2,1,0:T(8,128)}, f32[5,128,256]{2,1,0:T(8,128)}, u32[]{:S(2)}, u32[]{:S(2)}) collective-permute-start(f32[5,128,256]{2,1,0:T(8,128)} %get-tuple-element.49), channel_id=1, source_target_pairs={{0,8},{8,0},{16,24},{24,16},{1,9},{9,1},{17,25},{25,17},{2,10},{10... | collective-permute-start | bytes 1966088 | tf_op jit(solution)/shard_map/ppermute | solution.py:532
  58.3 36.0 %collective-permute-start.8 = (f32[2,768,256]{2,1,0:T(8,128)}, f32[2,768,256]{2,1,0:T(8,128)}, u32[]{:S(2)}, u32[]{:S(2)}) collective-permute-start(f32[2,768,256]{2,1,0:T(8,128)} %get-tuple-element.53), channel_id=1, source_target_pairs={{0,1},{1,2},{2,3},{3,4},{4,5},{5,6},{6,7},{8,9},{9,10},{10,11},{11... | collective-permute-start | bytes 4718600 | tf_op jit(solution)/shard_map/ppermute | solution.py:527
  61.4 14.3 %collective-permute-start.9 = (f32[2,256,512]{2,1,0:T(8,128)}, f32[2,256,512]{2,1,0:T(8,128)S(1)}, u32[]{:S(2)}, u32[]{:S(2)}) collective-permute-start(f32[2,256,512]{2,1,0:T(8,128)} %get-tuple-element.54), channel_id=1, source_target_pairs={{0,8},{8,16},{16,24},{1,9},{9,17},{17,25},{2,10},{10,18},{18,26},{... | collective-permute-start | bytes 3145736 | tf_op jit(solution)/shard_map/ppermute | solution.py:527
  63.1 4.3 %copy-start.8 = (f32[2,2,256,256]{3,2,1,0:T(8,128)S(1)}, f32[2,2,256,256]{3,2,1,0:T(8,128)}, u32[]{:S(2)}) copy-start(f32[2,2,256,256]{3,2,1,0:T(8,128)} %probe.1) | copy-start | bytes 3145732
  64.6 11.0 %collective-permute-start.7 = (f32[5,64,256]{2,1,0:T(8,128)S(1)}, f32[5,64,256]{2,1,0:T(8,128)S(1)}, u32[]{:S(2)}, u32[]{:S(2)}) collective-permute-start(f32[5,64,256]{2,1,0:T(8,128)S(1)} %constant_dynamic-slice_fusion), channel_id=1, source_target_pairs={{0,16},{8,24},{16,0},{24,8},{1,17},{9,25},{17,1},{25,9},{2,18},{10... | collective-permute-start | bytes 983048 | tf_op jit(solution)/shard_map/ppermute | solution.py:532
  95.1 15.4 %all-to-all-start = ((f32[8,5,8,256]{3,2,1,0:T(8,128)}), f32[8,5,8,256]{3,2,1,0:T(8,128)S(1)}, u32[]{:S(2)}, u32[]{:S(2)}) async-start(f32[8,5,8,256]{3,2,1,0:T(8,128)} %copy_bitcast_fusion), calls=%async_computation | async-start | bytes 655360 | tf_op jit(solution)/shard_map/all_to_all | solution.py:644
  112.0 12.1 %all-to-all-start.1 = ((f32[8,4,8,256]{3,2,1,0:T(8,128)}), f32[8,4,8,256]{3,2,1,0:T(8,128)S(1)}, u32[]{:S(2)}, u32[]{:S(2)}) async-start(f32[8,4,8,256]{3,2,1,0:T(8,128)} %broadcast_in_dim.2), calls=%async_computation.1 | async-start | bytes 524288 | tf_op jit(solution)/shard_map/all_to_all | solution.py:650
  117.5 6.7 %collective-permute-start.10 = (f32[2,256,256]{2,1,0:T(8,128)}, f32[2,256,256]{2,1,0:T(8,128)}, u32[]{:S(2)}, u32[]{:S(2)}) collective-permute-start(f32[2,256,256]{2,1,0:T(8,128)} %slice.19), channel_id=1, source_target_pairs={{0,8},{8,16},{16,24},{1,9},{9,17},{17,25},{2,10},{10,18},{18,26},{... | collective-permute-start | bytes 1572872 | tf_op jit(solution)/shard_map/ppermute | solution.py:527
  124.2 25.9 %collective-permute-start.11 = (f32[4,64,256]{2,1,0:T(8,128)S(1)}, f32[4,64,256]{2,1,0:T(8,128)S(1)}, u32[]{:S(2)}, u32[]{:S(2)}) collective-permute-start(f32[4,64,256]{2,1,0:T(8,128)S(1)} %copy_bitcast_fusion.1.mine), channel_id=1, source_target_pairs={{0,16},{8,24},{16,0},{24,8},{1,17},{9,25},{17,1},{25,9},{2,18},{10... | collective-permute-start | bytes 786440 | tf_op jit(solution)/shard_map/ppermute | solution.py:532
  143.2 1.6 %copy-start.3 = (f32[2,512,512]{2,1,0:T(8,128)S(1)}, f32[2,512,512]{2,1,0:T(8,128)}, u32[]{:S(2)}) copy-start(f32[2,512,512]{2,1,0:T(8,128)} %copy-done.2) | copy-start | bytes 6291460
  144.8 1.2 copy-start.5
  150.1 2.0 %collective-permute-start.12 = (f32[4,128,256]{2,1,0:T(8,128)S(1)}, f32[4,128,256]{2,1,0:T(8,128)S(1)}, u32[]{:S(2)}, u32[]{:S(2)}) collective-permute-start(f32[4,128,256]{2,1,0:T(8,128)S(1)} %join.2.mine), channel_id=1, source_target_pairs={{0,8},{8,0},{16,24},{24,16},{1,9},{9,1},{17,25},{25,17},{2,10},{10... | collective-permute-start | bytes 1572872 | tf_op jit(solution)/shard_map/ppermute | solution.py:532
  (2 other events, 2.0 us)

commit v2 on v1

--- a/solution.py
+++ b/solution.py
@@ -13,6 +13,8 @@
 F32 = jnp.float32
 BF16 = jnp.bfloat16
 MIB = 1024 * 1024
+LONG = pl.CostEstimate(flops=30_000_000_000, bytes_accessed=4_000_000, transcendentals=0)
+SHORT = pl.CostEstimate(flops=0, bytes_accessed=1_000_000, transcendentals=0)
 FLOOR = 0.3
 
 
@@ -37,11 +39,8 @@
     return forward, np.ascontiguousarray(forward.transpose(0, 1, 3, 2))
 
 
-def order_tables(length):
-    order = np.concatenate([np.arange(0, length, 2), np.arange(1, length, 2)])
-    table = np.eye(length)[order]
-    rows = np.concatenate([table] * 3, axis=1)
-    return rows.astype(ml_dtypes.bfloat16), rows.T.astype(ml_dtypes.bfloat16)
+def in_hbm(array):
+    return pltpu.with_memory_space_constraint(array, pltpu.HBM)
 
 
 def dot(a, b):
@@ -51,6 +50,18 @@
 def split(x):
     high = x.astype(BF16)
     return high, (x - high.astype(F32)).astype(BF16)
+
+
+def roll_rows(x, shift):
+    return pltpu.roll(x.reshape(x.shape[0] // 8, 8, x.shape[1]), shift, 1)
+
+
+def roll_rows(x, shift):
+    return pltpu.roll(x.reshape(x.shape[0] // 8, 8, x.shape[1]), shift, 1)
+
+
+def roll_rows(x, shift):
+    return pltpu.roll(x.reshape(x.shape[0] // 8, 8, x.shape[1]), shift, 1)
 
 
 def roll_rows(x, shift):
@@ -156,30 +167,67 @@
             pltpu.VMEM((tile_shape[0] + 2 * size, tile_shape[1] + 2 * size), F32),
         ],
         compiler_params=pltpu.CompilerParams(vmem_limit_bytes=8 * MIB),
-        cost_estimate=pl.CostEstimate(flops=4_000_000_000, bytes_accessed=16_000_000, transcendentals=0),
+        cost_estimate=pl.CostEstimate(flops=4_000_000_000, bytes_accessed=1_000_000, transcendentals=0),
         name="light",
     )(meta, probe)
 
 
-def arrange_kernel(meta, amplitudes, order_rows, order_cols, out):
-    @pl.loop(0, meta[0, 2 * amplitudes.shape[0]])
+def arrange_kernel(meta, amplitudes, out, given, moved, in_sems, out_sems):
+    slots, size, _ = amplitudes.shape
+    count = meta[0, 2 * slots]
+
+    def load(slot):
+        return pltpu.make_async_copy(amplitudes.at[slot], given.at[slot], in_sems.at[slot])
+
+    def store(slot):
+        return pltpu.make_async_copy(moved.at[slot], out.at[slot], out_sems.at[slot])
+
+    @pl.loop(0, count)
     def _(slot):
-        x = dot(order_rows[...], jnp.concatenate(split_three(amplitudes[slot]), axis=0))
-        out[slot] = dot(jnp.concatenate(split_three(x), axis=1), order_cols[...])
+        load(slot).start()
+
+    first = lax.broadcasted_iota(jnp.int32, (size, size), 0)
+    second = lax.broadcasted_iota(jnp.int32, (size, size), 1)
+    half = size // 2
+
+    def source(index):
+        return jnp.where(index < half, 2 * index, 2 * index - (size - 1))
+
+    rows = (source(first) == second).astype(F32).astype(BF16)
+    cols = (source(second) == first).astype(F32).astype(BF16)
+    rows = jnp.concatenate([rows, rows], axis=1)
+    cols = jnp.concatenate([cols, cols], axis=0)
+
+    @pl.loop(0, count)
+    def _(slot):
+        load(slot).wait()
+        x = dot(rows, jnp.concatenate(split(given[slot]), axis=0))
+        moved[slot] = dot(jnp.concatenate(split(x), axis=1), cols)
+        store(slot).start()
+
+    @pl.loop(0, count)
+    def _(slot):
+        store(slot).wait()
 
 
 def arrange(meta, amplitudes):
-    order_rows, order_cols = (jnp.asarray(table) for table in order_tables(amplitudes.shape[2]))
-    vmem = pl.BlockSpec(memory_space=pltpu.VMEM)
+    slots = amplitudes.shape[0]
+    hbm = pl.BlockSpec(memory_space=pltpu.HBM)
     return pl.pallas_call(
         arrange_kernel,
-        out_shape=jax.ShapeDtypeStruct(amplitudes.shape, F32),
-        in_specs=[pl.BlockSpec(memory_space=pltpu.SMEM)] + [vmem] * 3,
-        out_specs=vmem,
+        out_shape=pltpu.HBM(amplitudes.shape, F32),
+        in_specs=[pl.BlockSpec(memory_space=pltpu.SMEM), hbm],
+        out_specs=hbm,
+        scratch_shapes=[
+            pltpu.VMEM(amplitudes.shape, F32),
+            pltpu.VMEM(amplitudes.shape, F32),
+            pltpu.SemaphoreType.DMA((slots,)),
+            pltpu.SemaphoreType.DMA((slots,)),
+        ],
         compiler_params=pltpu.CompilerParams(vmem_limit_bytes=8 * MIB),
-        cost_estimate=pl.CostEstimate(flops=2_000_000_000, bytes_accessed=8_000_000, transcendentals=0),
+        cost_estimate=LONG,
         name="arrange",
-    )(meta, amplitudes, order_rows, order_cols)
+    )(meta, in_hbm(amplitudes))
 
 
 def three_left(table, t):
@@ -201,8 +249,8 @@
 
 
 def slots_kernel(
-    needs_rim, meta, probe, amplitudes, sources, forward_t, backward_t, init, outs, probe_out,
-    ext, grid, chosen, patch_f, patch_b, x_f, y_f, z_f, g_s, x_b, z_b, back, template, sems,
+    needs_rim, meta, probe, amplitudes, sources, forward_h, backward_h, init, note, outs, probe_out,
+    ext, grid, amp, forward_t, backward_t, chosen, patch_f, patch_b, x_f, y_f, z_f, g_s, x_b, z_b, back, template, sums, sems,
 ):
     size = probe.shape[2]
     half = size // 2
@@ -210,7 +258,11 @@
     slots = amplitudes.shape[0]
     tile_rows, tile_cols = (n - size for n in ext.shape[1:])
     step = 32
-    load_sems, out_sems = sems
+    fine = 16
+    load_sems, amp_sems, out_sems = sems
+    sums_out = probe_out
+    if not needs_rim:
+        probe_out = sums
 
     regions = (
         (pl.ds(0, tile_rows), pl.ds(0, tile_cols)),
@@ -223,12 +275,17 @@
         pltpu.make_async_copy(source, ext.at[:, rows, cols], load_sems.at[i])
         for i, (source, (rows, cols)) in enumerate(zip(sources, regions))
     ]
+    loads.append(pltpu.make_async_copy(forward_h, forward_t, load_sems.at[7]))
+    loads.append(pltpu.make_async_copy(backward_h, backward_t, load_sems.at[8]))
     if needs_rim:
         loads.append(pltpu.make_async_copy(init[0], grid.at[:, :, pl.ds(0, tile_cols)], load_sems.at[5]))
         loads.append(pltpu.make_async_copy(init[1], probe_out, load_sems.at[6]))
     for load in loads:
         load.start()
 
+    def amp_copy(slot):
+        return pltpu.make_async_copy(amplitudes.at[slot], amp.at[slot], amp_sems.at[slot])
+
     def choose(slot, found):
         beyond = meta[0, 2 * slot + 1] + size > tile_cols
         wanted = beyond if needs_rim else jnp.logical_not(beyond)
@@ -236,6 +293,7 @@
         @pl.when(wanted)
         def _():
             chosen[found] = slot
+            amp_copy(slot).start()
 
         return found + wanted.astype(jnp.int32)
 
@@ -283,12 +341,12 @@
             cols = pl.ds(m * size, size)
             parts = []
             for base in (at, half + at):
-                rows = pl.ds(base, step)
+                rows = pl.ds(base, fine)
                 pr, pi = patch_f[0, rows, :], patch_f[1, rows, :]
                 qr, qi = probe[m, 0, rows, :], probe[m, 1, rows, :]
                 parts.append((qr * pr - qi * pi, qr * pi + qi * pr))
             for c in range(2):
-                rows = pl.ds(c * half + at, step)
+                rows = pl.ds(c * half + at, fine)
                 for t, value in enumerate((parts[0][c] + parts[1][c], parts[0][c] - parts[1][c])):
                     x_f[t, 0, rows, cols], x_f[t, 1, rows, cols] = split(value)
 
@@ -312,23 +370,25 @@
             )
 
         def scale(v, at):
-            waves = [z_f[v, pl.ds(m * size + at, step), :] for m in range(modes)]
-            total = jnp.zeros((step, half), F32)
+            if v == 0 and at == 0:
+                amp_copy(slot).wait()
+            waves = [z_f[v, pl.ds(m * size + at, fine), :] for m in range(modes)]
+            total = jnp.zeros((fine, half), F32)
             for wave in waves:
                 total += wave[:, :half] * wave[:, :half] + wave[:, half:] * wave[:, half:]
-            measured = amplitudes[slot, pl.ds(at, step), pl.ds(v * half, half)]
+            measured = amp[slot, pl.ds(at, fine), pl.ds(v * half, half)]
             factor = measured * lax.rsqrt(jnp.maximum(total, FLOOR * FLOOR)) - 1.0
             factor = jnp.concatenate([factor, factor], axis=1)
             for m in range(modes):
-                rows = pl.ds(m * size + at, step)
+                rows = pl.ds(m * size + at, fine)
                 g_s[v, 0, rows, :], g_s[v, 1, rows, :] = split(waves[m] * factor)
 
         pieces = [(take, at) for at in range(0, size, step)]
         for m in range(modes):
-            pieces += [(fold_rows, m, at) for at in range(0, half, step)]
+            pieces += [(fold_rows, m, at) for at in range(0, half, fine)]
             pieces += [(dft_rows, m, t) for t in range(2)]
             pieces += [(dft_cols, m, v) for v in range(2)]
-        pieces += [(scale, v, at) for v in range(2) for at in range(0, size, step)]
+        pieces += [(scale, v, at) for v in range(2) for at in range(0, size, fine)]
         return [functools.partial(*piece) for piece in pieces]
 
     def backward(slot):
@@ -362,15 +422,15 @@
             for m in range(modes):
                 pair = []
                 for c in range(2):
-                    rows = pl.ds(c * half + at, step)
+                    rows = pl.ds(c * half + at, fine)
                     even, odd = back[m, 0, rows, :], back[m, 1, rows, :]
                     pair.append((even + odd, even - odd))
                 waves.append(pair)
             for h in range(2):
-                rows = pl.ds(h * half + at, step)
+                rows = pl.ds(h * half + at, fine)
                 pr, pi = patch_b[0, rows, :], patch_b[1, rows, :]
-                grad_r = jnp.zeros((step, size), F32)
-                grad_i = jnp.zeros((step, size), F32)
+                grad_r = jnp.zeros((fine, size), F32)
+                grad_i = jnp.zeros((fine, size), F32)
                 for m in range(modes):
                     br, bi = waves[m][0][h], waves[m][1][h]
                     qr, qi = probe[m, 0, rows, :], probe[m, 1, rows, :]
@@ -378,7 +438,7 @@
                     grad_i += qr * bi - qi * br
                     probe_out[2 * m, rows, :] += pr * br + pi * bi
                     probe_out[2 * m + 1, rows, :] += pr * bi - pi * br
-                spot = pl.ds(8 + h * half + at, step)
+                spot = pl.ds(8 + h * half + at, fine)
                 template[0, spot, :] = grad_r
                 template[1, spot, :] = grad_i
 
@@ -391,7 +451,7 @@
         for m in range(modes):
             pieces += [(unfold_cols, m, t, at) for t in range(2) for at in range(0, half, step)]
             pieces += [(dft_rows, m, t) for t in range(2)]
-        pieces += [(gradients, at) for at in range(0, half, step)]
+        pieces += [(gradients, at) for at in range(0, half, fine)]
         pieces += [(add, c) for c in range(2)]
         return [functools.partial(*piece) for piece in pieces]
 
@@ -414,14 +474,27 @@
         weave(backward(chosen[count - 1]), [])
 
     if needs_rim:
+        top, bottom, rest = pl.ds(0, size), pl.ds(size, tile_rows - size), pl.ds(tile_cols, size)
+        note_rows = pl.ds(size, 8)
         parts = [
             grid.at[:, pl.ds(0, tile_rows), pl.ds(0, tile_cols)],
-            grid.at[:, :, pl.ds(tile_cols, size)],
-            grid.at[:, pl.ds(tile_rows, size), pl.ds(0, tile_cols)],
-            probe_out.at[:, pl.ds(pl.multiple_of(meta[0, 2 * slots + 1] * half, half), half)],
+            grid.at[:, bottom, rest],
+            grid.at[:, top, rest],
+            grid.at[:, pl.ds(tile_rows, size), :],
+            note[0],
+            note[0],
+        ]
+        outs = [
+            outs[0],
+            outs[1],
+            outs[2].at[:, top],
+            outs[3].at[:, top],
+            outs[2].at[0, note_rows],
+            outs[3].at[0, note_rows, pl.ds(0, size)],
         ]
     else:
-        parts = [grid.at[:, :, pl.ds(0, tile_cols)]]
+        parts = [grid.at[:, :, pl.ds(0, tile_cols)], sums]
+        outs = [*outs, sums_out]
     stores = [pltpu.make_async_copy(part, out, out_sems.at[i]) for i, (part, out) in enumerate(zip(parts, outs))]
     for store in stores:
         store.start()
@@ -429,7 +502,7 @@
         store.wait()
 
 
-def visit_slots(meta, probe, amplitudes, sources, init):
+def visit_slots(meta, probe, amplitudes, sources, init, note=()):
     size = probe.shape[2]
     modes = probe.shape[0]
     slots = amplitudes.shape[0]
@@ -437,33 +510,38 @@
     tables = [jnp.asarray(item) for item in dft_tables(size)]
     vmem = pl.BlockSpec(memory_space=pltpu.VMEM)
     anywhere = pl.BlockSpec(memory_space=pl.ANY)
+    hbm = pl.BlockSpec(memory_space=pltpu.HBM)
     needs_rim = bool(init)
     if needs_rim:
-        shapes = [(2, rows, cols), (2, rows + size, size), (2, size, cols), (2 * modes + 1, size // 2, size)]
+        shapes = [(2, rows, cols), (2, rows - size, size), (2, size + 8, size), (2, size + 8, cols + size)]
     else:
         shapes = [(2, rows + size, cols)]
-    splits = np.cumsum([1, 1, 1, len(sources), 1, 1, len(init), len(shapes), 1])
+    splits = np.cumsum([1, 1, 1, len(sources), 1, 1, len(init), len(note), len(shapes), 1])
 
     def kernel(*refs):
-        meta, probe, amplitudes, sources, forward_t, backward_t, init, outs, probe_out = (
+        meta, probe, amplitudes, sources, forward_t, backward_t, init, note, outs, probe_out = (
             refs[a:b] for a, b in zip([0, *splits[:-1]], splits)
         )
         scratch = refs[splits[-1] :]
         slots_kernel(
-            needs_rim, meta[0], probe[0], amplitudes[0], sources, forward_t[0], backward_t[0], init, outs,
-            probe_out[0], *scratch[:-2], scratch[-2:],
+            needs_rim, meta[0], probe[0], amplitudes[0], sources, forward_t[0], backward_t[0], init, note, outs,
+            probe_out[0], *scratch[:-3], scratch[-3:],
         )
 
     return pl.pallas_call(
         kernel,
-        out_shape=[jax.ShapeDtypeStruct(shape, F32) for shape in shapes]
-        + [jax.ShapeDtypeStruct((2 * modes + 1, size, size), F32)],
-        in_specs=[pl.BlockSpec(memory_space=pltpu.SMEM), vmem, vmem] + [anywhere] * len(sources)
-        + [vmem] * 2 + [anywhere] * len(init),
-        out_specs=[anywhere] * len(shapes) + [vmem],
+        out_shape=[pltpu.HBM(shapes[0], F32)]
+        + [jax.ShapeDtypeStruct(shape, F32) for shape in shapes[1:]]
+        + [(jax.ShapeDtypeStruct if needs_rim else pltpu.HBM)((2 * modes + 1, size, size), F32)],
+        in_specs=[pl.BlockSpec(memory_space=pltpu.SMEM), vmem, hbm, hbm] + [anywhere] * (len(sources) - 1)
+        + [hbm] * (2 + len(init)) + [anywhere] * len(note),
+        out_specs=[hbm] + [anywhere] * (len(shapes) - 1) + [vmem if needs_rim else hbm],
         scratch_shapes=[
             pltpu.VMEM((2, rows + size, cols + size), F32),
             pltpu.VMEM((2, rows + size, cols + size), F32),
+            pltpu.VMEM(amplitudes.shape, F32),
+            pltpu.VMEM(tables[0].shape, BF16),
+            pltpu.VMEM(tables[1].shape, BF16),
             pltpu.SMEM((slots,), jnp.int32),
             pltpu.VMEM((2, size, size), F32),
             pltpu.VMEM((2, size, size), F32),
@@ -475,50 +553,84 @@
             pltpu.VMEM((2, modes * size, size), F32),
             pltpu.VMEM((modes, 2, size, size), F32),
             pltpu.VMEM((2, size + 16, size), F32),
-            pltpu.SemaphoreType.DMA((7,)),
-            pltpu.SemaphoreType.DMA((4,)),
+            pltpu.VMEM((8, 128) if needs_rim else (2 * modes + 1, size, size), F32),
+            pltpu.SemaphoreType.DMA((9,)),
+            pltpu.SemaphoreType.DMA((slots,)),
+            pltpu.SemaphoreType.DMA((6,)),
         ],
         compiler_params=pltpu.CompilerParams(vmem_limit_bytes=28 * MIB),
         cost_estimate=pl.CostEstimate(flops=12_000_000_000, bytes_accessed=16_000_000, transcendentals=0),
         name="slots_beyond" if needs_rim else "slots_inside",
-    )(meta, probe, amplitudes, *sources, *tables, *init)
-
-
-def finish_kernel(own, right, lower, corner, inverse_light, tile, out):
-    size = right.shape[2]
-    step = pl.program_id(0)
-    scale = inverse_light[...]
-    spill = jnp.where(step < size // own.shape[1], 1.0, 0.0)
-    for c in range(2):
-        near = own[c, :, :size] + right[c] + spill * (lower[c, :, :size] + corner[c])
-        far = own[c, :, size:] + spill * lower[c, :, size:]
-        out[c, :, :size] = tile[c, :, :size] + near * scale[:, :size]
-        out[c, :, size:] = tile[c, :, size:] + far * scale[:, size:]
-
-
-def finish(own, right, lower, corner, inverse_light, tile):
+    )(meta, probe, in_hbm(amplitudes), in_hbm(sources[0]), *sources[1:], *map(in_hbm, tables), *map(in_hbm, init), *note)
+
+
+def finish_kernel(
+    own, top, bottom, lower, scale, tile, out, own_s, right_s, lower_s, scale_s, tile_s, in_sems, out_sems
+):
+    size = right_s.shape[2]
+    block = 128
+    blocks = own_s.shape[1] // block
+
+    def copies(i):
+        rows = pl.ds(i * block, block)
+        pairs = [
+            (own.at[:, rows], own_s.at[:, rows]),
+            (scale.at[rows], scale_s.at[rows]),
+            (tile.at[:, rows], tile_s.at[:, rows]),
+        ]
+        if i < size // block:
+            pairs.append((top.at[:, rows], right_s.at[:, rows]))
+            pairs.append((lower.at[:, rows, pl.ds(0, lower_s.shape[2])], lower_s.at[:, rows]))
+        else:
+            pairs.append((bottom.at[:, pl.ds(i * block - size, block)], right_s.at[:, rows]))
+        return [pltpu.make_async_copy(a, b, in_sems.at[i, k]) for k, (a, b) in enumerate(pairs)]
+
+    loads = [copies(i) for i in range(blocks)]
+    for load in loads:
+        for copy in load:
+            copy.start()
+    stores = []
+    for i in range(blocks):
+        for copy in loads[i]:
+            copy.wait()
+        rows = pl.ds(i * block, block)
+        for at in range(i * block, (i + 1) * block, 32):
+            part = pl.ds(at, 32)
+            for c in range(2):
+                near, far = own_s[c, part, :size] + right_s[c, part, :], own_s[c, part, size:]
+                if i < size // block:
+                    near, far = near + lower_s[c, part, :size], far + lower_s[c, part, size:]
+                own_s[c, part, :size] = tile_s[c, part, :size] + near * scale_s[part, :size]
+                own_s[c, part, size:] = tile_s[c, part, size:] + far * scale_s[part, size:]
+        stores.append(pltpu.make_async_copy(own_s.at[:, rows], out.at[:, rows], out_sems.at[i]))
+        stores[-1].start()
+    for store in stores:
+        store.wait()
+
+
+def finish(own, top, bottom, lower, inverse_light, tile):
     rows, cols = tile.shape[1:]
-    size = right.shape[2]
-    block = 128
-    last = size // block - 1
-    whole = pl.BlockSpec((2, block, cols), lambda i: (0, i, 0))
+    size = top.shape[2]
+    anywhere = pl.BlockSpec(memory_space=pl.ANY)
+    hbm = pl.BlockSpec(memory_space=pltpu.HBM)
     return pl.pallas_call(
         finish_kernel,
-        grid=(rows // block,),
         out_shape=jax.ShapeDtypeStruct(tile.shape, F32),
-        in_specs=[
-            whole,
-            pl.BlockSpec((2, block, size), lambda i: (0, i, 0)),
-            pl.BlockSpec((2, block, cols), lambda i: (0, jnp.minimum(i, last), 0)),
-            pl.BlockSpec((2, block, size), lambda i: (0, jnp.minimum(i, last), 0)),
-            pl.BlockSpec((block, cols), lambda i: (i, 0)),
-            whole,
+        in_specs=[hbm] + [anywhere] * 4 + [hbm],
+        out_specs=hbm,
+        scratch_shapes=[
+            pltpu.VMEM(tile.shape, F32),
+            pltpu.VMEM((2, rows, size), F32),
+            pltpu.VMEM((2, size, cols), F32),
+            pltpu.VMEM((rows, cols), F32),
+            pltpu.VMEM(tile.shape, F32),
+            pltpu.SemaphoreType.DMA((rows // 128, 5)),
+            pltpu.SemaphoreType.DMA((rows // 128,)),
         ],
-        out_specs=whole,
-        compiler_params=pltpu.CompilerParams(vmem_limit_bytes=8 * MIB),
+        compiler_params=pltpu.CompilerParams(vmem_limit_bytes=10 * MIB),
         cost_estimate=pl.CostEstimate(flops=3_000_000, bytes_accessed=12_000_000, transcendentals=0),
         name="finish",
-    )(own, right, lower, corner, inverse_light, tile)
+    )(in_hbm(own), top, bottom, lower, inverse_light, in_hbm(tile))
 
 
 def from_behind(array, axis, by):
@@ -536,10 +648,7 @@
     return lax.optimization_barrier(arrays)
 
 
-def cut(tile, size):
-    rows, cols = tile.shape[1:]
-    regions = ((0, size, size), (0, size, cols), (size, rows - size, size))
-
+def cut(tile, regions, cost, name):
     def kernel(tile, *refs):
         sems = refs[-1]
         copies = [
@@ -551,17 +660,94 @@
         for copy in copies:
             copy.wait()
 
+    return pl.pallas_call(
+        kernel,
+        out_shape=[jax.ShapeDtypeStruct((2, height, width), F32) for _, height, width in regions],
+        in_specs=[pl.BlockSpec(memory_space=pltpu.HBM)],
+        out_specs=[pl.BlockSpec(memory_space=pltpu.VMEM)] * len(regions),
+        scratch_shapes=[pltpu.SemaphoreType.DMA((len(regions),))],
+        compiler_params=pltpu.CompilerParams(vmem_limit_bytes=4 * MIB),
+        cost_estimate=cost,
+        name=name,
+    )(in_hbm(tile))
+
+
+def pick(share, index):
+    half = share.shape[1] // 2
+
+    def kernel(index, share, out, sem):
+        rows = pl.ds(pl.multiple_of(index[0] * half, half), half)
+        copy = pltpu.make_async_copy(share.at[:, rows], out, sem.at[0])
+        copy.start()
+        copy.wait()
+
     anywhere = pl.BlockSpec(memory_space=pl.ANY)
     return pl.pallas_call(
         kernel,
-        out_shape=[jax.ShapeDtypeStruct((2, height, width), F32) for _, height, width in regions],
-        in_specs=[anywhere],
-        out_specs=[anywhere] * len(regions),
-        scratch_shapes=[pltpu.SemaphoreType.DMA((len(regions),))],
+        out_shape=jax.ShapeDtypeStruct((share.shape[0], half, share.shape[2]), F32),
+        in_specs=[pl.BlockSpec(memory_space=pltpu.SMEM), anywhere],
+        out_specs=anywhere,
+        scratch_shapes=[pltpu.SemaphoreType.DMA((1,))],
         compiler_params=pltpu.CompilerParams(vmem_limit_bytes=MIB),
-        cost_estimate=pl.CostEstimate(flops=0, bytes_accessed=4_000_000, transcendentals=0),
-        name="cut",
-    )(tile)
+        cost_estimate=LONG,
+        name="pick",
+    )(index.reshape(1), share)
+
+
+def fold(mine, index, got, upper):
+    count, half, width = got.shape
+    quarter = half // 2
+
+    def kernel(place, mine, got, send, keep):
+        for k, out in ((1 - place[1], send), (place[1], keep)):
+            for c in range(count):
+                out[c] = (
+                    mine[c, pl.ds(pl.multiple_of(place[0] * half + k * quarter, quarter), quarter), :]
+                    + got[c, pl.ds(pl.multiple_of(k * quarter, quarter), quarter), :]
+                )
+
+    vmem = pl.BlockSpec(memory_space=pltpu.VMEM)
+    shape = jax.ShapeDtypeStruct((count, quarter, width), F32)
+    return pl.pallas_call(
+        kernel,
+        out_shape=[shape, shape],
+        in_specs=[pl.BlockSpec(memory_space=pltpu.SMEM), vmem, vmem],
+        out_specs=[vmem, vmem],
+        compiler_params=pltpu.CompilerParams(vmem_limit_bytes=6 * MIB),
+        cost_estimate=SHORT,
+        name="fold",
+    )(jnp.stack([index, upper]), mine, got)
+
+
+def merge(right, lower):
+    _, height, size = right.shape
+    rows = height - 8
+    cols = lower.shape[2] - size
+
+    def kernel(right, lower, out, corner, sems):
+        copies = [
+            pltpu.make_async_copy(lower.at[:, pl.ds(0, rows), pl.ds(cols, size)], corner, sems.at[0]),
+            pltpu.make_async_copy(lower.at[0, pl.ds(rows, 8), pl.ds(0, size)], out.at[1, pl.ds(rows, 8)], sems.at[1]),
+        ]
+        for copy in copies:
+            copy.start()
+        out[0, rows:, :] = right[0, rows:, :]
+        for copy in copies:
+            copy.wait()
+        for c in range(2):
+            out[c, :rows, :] = right[c, :rows, :] + corner[c]
+
+    vmem = pl.BlockSpec(memory_space=pltpu.VMEM)
+    return pl.pallas_call(
+        kernel,
+        out_shape=jax.ShapeDtypeStruct(right.shape, F32),
+        in_specs=[vmem, pl.BlockSpec(memory_space=pl.ANY)],
+        out_specs=vmem,
+        scratch_shapes=[pltpu.VMEM((2, rows, size), F32), pltpu.SemaphoreType.DMA((2,))],
+        compiler_params=pltpu.CompilerParams(vmem_limit_bytes=4 * MIB),
+        cost_estimate=SHORT,
+        name="merge",
+    )(right, lower)
 
 
 def join(upper, mine, other):
@@ -601,59 +787,62 @@
     def relative(table):
         return jnp.concatenate([table[:, : 2 * slots] - jnp.tile(origin, slots)[None], table[:, 2 * slots :]], axis=1)
 
-    right_up, lower, rest = cut(object_field, size)
+    right_up, right_down = cut(
+        object_field, ((0, size, size), (size, tile_rows - size, size)), SHORT, "cut_right"
+    )
+    right_up, right_down, after_right = together(right_up, right_down, object_field)
     right_up = from_behind(right_up, "col", -1)
+    right_down = from_behind(right_down, "col", -1)
+    (lower,) = cut(after_right, ((0, size, tile_cols),), LONG, "cut_lower")
+    meta = jnp.concatenate([positions.reshape(1, 2 * slots), counts.reshape(1, 1)], axis=1)
     lower = from_behind(lower, "row", -1)
 
-    meta = jnp.concatenate([positions.reshape(1, 2 * slots), counts.reshape(1, 1)], axis=1)
-    mine = jnp.concatenate([relative(meta), (1 - uppers[0]).astype(jnp.int32).reshape(1, 1)], axis=1)
+    mine = relative(meta)
+    note = jnp.pad(meta.astype(F32), ((0, 7), (0, size - meta.shape[1])))
     amplitudes = arrange(mine, amplitudes)
-    amplitudes, rest = together(amplitudes, rest)
-    right_down = from_behind(rest, "col", -1)
-    table = jnp.concatenate([meta, from_behind(meta, "col", 1)], axis=0)
-    table = relative(jnp.concatenate([table, from_behind(table, "row", 1)], axis=0))
-    right_up, amplitudes, lower, table = together(right_up, amplitudes, lower, table)
+    right_up, amplitudes = together(right_up, amplitudes)
     corner = from_behind(right_up, "row", -1)
+    amplitudes, lower = together(amplitudes, lower)
     init = visit_slots(mine, probe, amplitudes, [object_field, lower], [])
     right_up, right_down, corner, *init = together(right_up, right_down, corner, *init)
-    own, right_spill, lower_spill, send, share = visit_slots(
-        mine, probe, amplitudes, [object_field, lower, right_up, right_down, corner], list(init)
+    own, bottom_spill, top_spill, lower_spill, share = visit_slots(
+        mine, probe, amplitudes, [object_field, lower, right_up, right_down, corner], list(init), [note]
     )
 
+    bottom_spill = from_behind(bottom_spill, "col", 1)
+    lower_spill = from_behind(lower_spill, "row", 1)
     start = jnp.zeros((), jnp.int32)
-    got = None
-    for bit, upper in zip(bits, uppers):
-        half = share.shape[1] // 2
-        if got is not None:
-            send = lax.dynamic_slice_in_dim(share, (1 - upper) * half, half, axis=1)
+    index = uppers[0]
+    send = pick(share, 1 - index)
+    for k, (bit, upper) in enumerate(zip(bits, uppers)):
         got = exchange(send, "row", bit)
-        if bit == bits[0]:
-            right_spill = from_behind(right_spill, "col", 1)
-            lower_spill = from_behind(lower_spill, "row", 1)
-        if bit == bits[-1]:
-            table, send = together(table, send)
-            inverse_light = light(table, probe, (tile_rows, tile_cols))
-            got, inverse_light = together(got, inverse_light)
-        share = lax.dynamic_slice_in_dim(share, upper * half, half, axis=1) + got
-        start = start + upper * half
+        start = start + upper * (size >> (k + 1))
+        if k + 1 < len(bits):
+            send, share = fold(share, index, got, uppers[k + 1])
+            index = jnp.zeros((), jnp.int32)
+    share = share + got
+    share, bottom_spill, lower_spill = together(share, bottom_spill, lower_spill)
+    top_spill = from_behind(merge(top_spill, lower_spill), "col", 1)
     parts = lax.axis_size("col")
     rows = share.shape[1] // parts
-    share, right_spill, lower_spill = together(share, right_spill, lower_spill)
-    corner_spill = from_behind(right_spill[:, tile_rows:], "row", 1)
     share = share.reshape(2 * modes + 1, parts, rows, size).transpose(1, 0, 2, 3)
     share = lax.all_to_all(share, "col", 0, 0, tiled=True).sum(axis=0)
     old = lax.dynamic_slice_in_dim(
         probe.reshape(2 * modes, size, size), start + lax.axis_index("col") * rows, rows, axis=1
     )
     new = old + share[: 2 * modes] / (share[2 * modes :] + 1.0)
+    new, top_spill = together(new, top_spill)
     new = jnp.broadcast_to(new[None], (parts,) + new.shape)
     new = lax.all_to_all(new, "col", 0, 0, tiled=True)
     new = new.transpose(1, 0, 2, 3).reshape(2 * modes, parts * rows, size)
-    new, corner_spill = together(new, corner_spill)
+    width = 2 * slots + 1
+    notes = [top_spill[:1, size], lower_spill[:1, size], top_spill[1:, size]]
+    table = jnp.concatenate([meta] + [item[:, :width].astype(jnp.int32) for item in notes], axis=0)
+    inverse_light = light(relative(table), probe, (tile_rows, tile_cols))
     for bit, upper in reversed(list(zip(bits, uppers))):
         other = exchange(new, "row", bit)
         if bit == bits[-1]:
-            new_object = finish(own, right_spill, lower_spill, corner_spill, inverse_light, object_field)
+            new_object = finish(own, top_spill, bottom_spill, lower_spill, inverse_light, object_field)
             other, new_object = together(other, new_object)
         new = join(upper, new, other)
     return (new_object, new.reshape(modes, 2, size, size))

time: 153 us -> 143 us (0.935); the launches traced: 153 us -> 140 us
  local copies, waits for them, and re-layouts: 19.1 us -> 6.02 us
  waiting for transfers between devices: 44.2 us -> 33 us
  starting transfers between devices: 57.5 us -> 64.4 us
  Pallas kernels: 27.4 us -> 33.9 us
  other arithmetic: 3.3 us -> 1.32 us
    ppermute x9 -> x7, waiting for transfers between devices: 22.7 us -> 10 us  [from_behind(): return lax.ppermute(array, axis, pairs)]
    unnamed x39 -> x17, local copies, waits for them, and re-layouts: 15.4 us -> 4.2 us
    ppermute x4, starting transfers between devices: 27.9 us -> 38.5 us  [exchange(): return lax.ppermute(array, axis, [(i, i ^ bit) for i in range(count)])]
    all_to_all x1, waiting for transfers between devices: 9.59 us -> 4.37 us  [body(): share = lax.all_to_all(share, 'col', 0, 0, tiled=True).sum(axis=0)]
    ppermute x9 -> x7, starting transfers between devices: 20.2 us -> 16 us  [from_behind(): return lax.ppermute(array, axis, pairs)]
    pallas_call x4 -> x7, Pallas kernels: 23.3 us -> 27 us  [the longest x2 17.9 us: visit_slots(): pl.pallas_call(kernel, out_shape=[pltpu.HBM(shapes[0], F32)] + [jax.Shape...]
    all_to_all x1, waiting for transfers between devices: 4.54 us -> 7.98 us  [body(): new = lax.all_to_all(new, 'col', 0, 0, tiled=True)]
    ppermute x4, waiting for transfers between devices: 7.39 us -> 10.6 us  [exchange(): return lax.ppermute(array, axis, [(i, i ^ bit) for i in range(count)])]
  transfers between devices with their start and end apart: 15 -> 13, of which waited for: 6 -> 7; matrix products, arithmetic and copies ran while one was open for 3% -> 1% of each run, Pallas kernels for 11% -> 15%
where the time goes in v2:
time: 143 us; the launch traced here: 140 us
  starting transfers between devices  64.4 us (45%)
  Pallas kernels  33.9 us (24%)
  waiting for transfers between devices  33 us (23%)
  local copies, waits for them, and re-layouts  6.02 us (4%)
  between operations  1.7 us (1%)
    ppermute x4, starting transfers between devices, exchange(): return lax.ppermute(array, axis, [(i, i ^ bit) for i in range(count)])  38.5 us
    pallas_call x2, Pallas kernels, visit_slots(): pl.pallas_call(kernel, out_shape=[pltpu.HBM(shapes[0], F32)] + [jax.Shape...  17.9 us
    ppermute x7, starting transfers between devices, from_behind(): return lax.ppermute(array, axis, pairs)  16 us
    ppermute x4, waiting for transfers between devices, exchange(): return lax.ppermute(array, axis, [(i, i ^ bit) for i in range(count)])  10.6 us
    ppermute x7, waiting for transfers between devices, from_behind(): return lax.ppermute(array, axis, pairs)  10 us
    all_to_all x1, waiting for transfers between devices, body(): new = lax.all_to_all(new, 'col', 0, 0, tiled=True)  7.98 us
    all_to_all x1, starting transfers between devices, body(): new = lax.all_to_all(new, 'col', 0, 0, tiled=True)  6.29 us
    pallas_call x2, Pallas kernels, cut(): pl.pallas_call(kernel, out_shape=[jax.ShapeDtypeStruct((2, height, width)...  4.41 us
  transfers between devices with their start and end apart: 13, of which 7 were waited for; matrix products, arithmetic and copies ran while one was open for 1% of the time, Pallas kernels for 15%

profile of v2, /device:TPU:0, one launch (start us, length us, event | category | flops | bytes accessed | tf_op | source)
XLA Modules:
  0.0 140.4 jit_solution(8646611454282283456)
XLA Ops:
  0.6 2.2 %cut_right.1 = (f32[2,256,256]{2,1,0:T(8,128)}, f32[2,256,256]{2,1,0:T(8,128)}) custom-call(f32[2,512,512]{2,1,0:T(8,128)} %tile.7), custom_call_target="tpu_custom_call" | custom-call | bytes 1000000 | tf_op jit(solution)/shard_map/cut_right/pallas_call | solution.py:663
  2.9 1.3 collective-permute-start
  4.2 1.3 collective-permute-start.2
  5.5 2.2 %cut_lower.1 = f32[2,256,512]{2,1,0:T(8,128)} custom-call(f32[2,512,512]{2,1,0:T(8,128)} %tile.7), custom_call_target="tpu_custom_call" | custom-call | flops 30000001024 | bytes 4000000 | tf_op jit(solution)/shard_map/cut_lower/pallas_call | solution.py:663
  7.7 1.3 collective-permute-start.1
  10.0 3.3 %arrange.1.refs_2_ = f32[8,256,256]{2,1,0:T(8,128)} custom-call(s32[1,17]{1,0:T(1,128)S(1)} %pad_add_fusion.4.meta.refs_0_, f32[8,256,256]{2,1,0:T(8,128)} %amplitudes.1), custom_call_target="tpu_custom_call" | custom-call | flops 30000001024 | bytes 4000000 | tf_op jit(solution)/shard_map/arrange/pallas_call | solution.py:216
  13.4 7.3 %collective-permute-done.refs_5_ = f32[2,256,256]{2,1,0:T(8,128)S(1)} collective-permute-done((f32[2,256,256]{2,1,0:T(8,128)}, f32[2,256,256]{2,1,0:T(8,128)S(1)}, u32[]{:S(2)}, u32[]{:S(2)}) %collective-permute-start) | collective-permute-done | bytes 524320 | tf_op jit(solution)/shard_map/ppermute | solution.py:639
  20.7 1.3 collective-permute-start.3
  22.0 8.2 %slots_inside.1 = (f32[2,768,512]{2,1,0:T(8,128)}, f32[5,256,256]{2,1,0:T(8,128)}) custom-call(s32[1,17]{1,0:T(1,128)S(1)} %pad_add_fusion.4.meta.refs_0_, f32[2,2,256,256]{3,2,1,0:T(8,128)S(1)} %copy-done, f32[8,256,256]{2,1,0:T(8,128)} %arrange.1.refs_2_, f32[2,512,512]{2,1,0:T(8,128)} %tile.7, f32[2,256,512]{2,1,0:T(8,128)S(1)} %collective-permute-done.1.refs_4_, ...), custom_call_target="tpu_custom_call" | custom-call | flops 12000000000 | bytes 16000000 | tf_op jit(solution)/shard_map/slots_inside/pallas_call | solution.py:531
  30.2 0.9 collective-permute-done.2.refs_6_
  31.9 1.0 copy-done.4
  32.9 1.0 copy-done.6
  34.0 9.7 %slots_beyond.1 = (f32[2,512,512]{2,1,0:T(8,128)}, f32[2,256,256]{2,1,0:T(8,128)}, f32[2,264,256]{2,1,0:T(8,128)S(1)}, f32[2,264,768]{2,1,0:T(8,128)}, f32[5,256,256]{2,1,0:T(8,128)S(1)}) custom-call(s32[1,17]{1,0:T(1,128)S(1)} %pad_add_fusion.4.meta.refs_0_, f32[2,2,256,256]{3,2,1,0:T(8,128)S(1)} %copy-done.1, f32[8,256,256]{2,1,0:T(8,128)} %arrange.1.refs_2_, ...), custom_call_target="tpu_custom_call" | custom-call | flops 12000000000 | bytes 16000000 | tf_op jit(solution)/shard_map/slots_beyond/pallas_call | solution.py:531
  43.7 4.7 %collective-permute-start.7 = (f32[2,264,768]{2,1,0:T(8,128)}, f32[2,264,768]{2,1,0:T(8,128)S(1)}, u32[]{:S(2)}, u32[]{:S(2)}) collective-permute-start(f32[2,264,768]{2,1,0:T(8,128)} %get-tuple-element.52), channel_id=1, source_target_pairs={{0,8},{8,16},{16,24},{1,9},{9,17},{17,25},{2,10},{10,18},{18,26},{... | collective-permute-start | bytes 4866056 | tf_op jit(solution)/shard_map/ppermute | solution.py:639
  48.5 0.9 pick.1
  49.3 18.7 %collective-permute-start.4 = (f32[5,128,256]{2,1,0:T(8,128)}, f32[5,128,256]{2,1,0:T(8,128)}, u32[]{:S(2)}, u32[]{:S(2)}) collective-permute-start(f32[5,128,256]{2,1,0:T(8,128)} %pick.1), channel_id=1, source_target_pairs={{0,8},{8,0},{16,24},{24,16},{1,9},{9,1},{17,25},{25,17},{2,10},{10... | collective-permute-start | bytes 1966088 | tf_op jit(solution)/shard_map/ppermute | solution.py:644
  68.0 2.1 %collective-permute-start.6 = (f32[2,256,256]{2,1,0:T(8,128)}, f32[2,256,256]{2,1,0:T(8,128)}, u32[]{:S(2)}, u32[]{:S(2)}) collective-permute-start(f32[2,256,256]{2,1,0:T(8,128)} %get-tuple-element.51), channel_id=1, source_target_pairs={{0,1},{1,2},{2,3},{3,4},{4,5},{5,6},{6,7},{8,9},{9,10},{10,11},{11... | collective-permute-start | bytes 1572872 | tf_op jit(solution)/shard_map/ppermute | solution.py:639
  70.2 1.2 fold.1
  71.3 1.3 collective-permute-start.5
  72.6 8.7 %collective-permute-done.5 = f32[5,64,256]{2,1,0:T(8,128)S(1)} collective-permute-done((f32[5,64,256]{2,1,0:T(8,128)S(1)}, f32[5,64,256]{2,1,0:T(8,128)S(1)}, u32[]{:S(2)}, u32[]{:S(2)}) %collective-permute-start.5) | collective-permute-done | bytes 327712 | tf_op jit(solution)/shard_map/ppermute | solution.py:644
  82.1 3.6 %all-to-all-start = ((f32[8,5,8,256]{3,2,1,0:T(8,128)}), f32[8,5,8,256]{3,2,1,0:T(8,128)S(1)}, u32[]{:S(2)}, u32[]{:S(2)}) async-start(f32[8,5,8,256]{3,2,1,0:T(8,128)} %copy_bitcast_fusion), calls=%async_computation | async-start | bytes 655360 | tf_op jit(solution)/shard_map/all_to_all | solution.py:829
  85.9 4.1 %collective-permute-start.8 = (f32[2,264,256]{2,1,0:T(8,128)S(1)}, f32[2,264,256]{2,1,0:T(8,128)S(1)}, u32[]{:S(2)}, u32[]{:S(2)}) collective-permute-start(f32[2,264,256]{2,1,0:T(8,128)S(1)} %merge.1), channel_id=1, source_target_pairs={{0,1},{1,2},{2,3},{3,4},{4,5},{5,6},{6,7},{8,9},{9,10},{10,11},{11... | collective-permute-start | bytes 1622024 | tf_op jit(solution)/shard_map/ppermute | solution.py:639
  90.0 4.4 %all-to-all-done = f32[8,5,8,256]{3,2,1,0:T(8,128)S(1)} async-done(((f32[8,5,8,256]{3,2,1,0:T(8,128)}), f32[8,5,8,256]{3,2,1,0:T(8,128)S(1)}, u32[]{:S(2)}, u32[]{:S(2)}) %all-to-all-start) | async-done | bytes 327712 | tf_op jit(solution)/shard_map/all_to_all | solution.py:829
  95.2 1.9 %collective-permute-done.8.top = f32[2,264,256]{2,1,0:T(8,128)S(1)} collective-permute-done((f32[2,264,256]{2,1,0:T(8,128)S(1)}, f32[2,264,256]{2,1,0:T(8,128)S(1)}, u32[]{:S(2)}, u32[]{:S(2)}) %collective-permute-start.8) | collective-permute-done | bytes 540704 | tf_op jit(solution)/shard_map/ppermute | solution.py:639
  97.8 6.3 %all-to-all-start.1 = ((f32[8,4,8,256]{3,2,1,0:T(8,128)}), f32[8,4,8,256]{3,2,1,0:T(8,128)S(1)}, u32[]{:S(2)}, u32[]{:S(2)}) async-start(f32[8,4,8,256]{3,2,1,0:T(8,128)} %broadcast_in_dim.2), calls=%async_computation.1 | async-start | bytes 524288 | tf_op jit(solution)/shard_map/all_to_all | solution.py:836
  104.3 8.0 %all-to-all-done.1 = f32[8,4,8,256]{3,2,1,0:T(8,128)S(1)} async-done(((f32[8,4,8,256]{3,2,1,0:T(8,128)}), f32[8,4,8,256]{3,2,1,0:T(8,128)S(1)}, u32[]{:S(2)}, u32[]{:S(2)}) %all-to-all-start.1) | async-done | bytes 262176 | tf_op jit(solution)/shard_map/all_to_all | solution.py:836
  112.3 18.5 %collective-permute-start.9 = (f32[4,64,256]{2,1,0:T(8,128)S(1)}, f32[4,64,256]{2,1,0:T(8,128)S(1)}, u32[]{:S(2)}, u32[]{:S(2)}) collective-permute-start(f32[4,64,256]{2,1,0:T(8,128)S(1)} %copy_bitcast_fusion.1.mine), channel_id=1, source_target_pairs={{0,16},{8,24},{16,0},{24,8},{1,17},{9,25},{17,1},{25,9},{2,18},{10... | collective-permute-start | bytes 786440 | tf_op jit(solution)/shard_map/ppermute | solution.py:644
  130.8 1.2 copy-done.2
  132.1 1.5 %light.1.scale = f32[512,512]{1,0:T(8,128)S(1)} custom-call(s32[4,17]{1,0:T(4,128)S(1)} %pad_add_fusion.1.meta, f32[2,2,256,256]{3,2,1,0:T(8,128)S(1)} %copy-done.2), custom_call_target="tpu_custom_call" | custom-call | flops 4000000000 | bytes 1000000 | tf_op jit(solution)/shard_map/light/pallas_call | solution.py:160
  133.6 3.6 %finish.1 = f32[2,512,512]{2,1,0:T(8,128)} custom-call(f32[2,512,512]{2,1,0:T(8,128)} %get-tuple-element.57.own, f32[2,264,256]{2,1,0:T(8,128)S(1)} %collective-permute-done.8.top, f32[2,256,256]{2,1,0:T(8,128)} %collective-permute-done.6.bottom, f32[2,264,768]{2,1,0:T(8,128)S(1)} %collective-permute-done.7.lower, f32[512,512]{1,0:T(8,128)S(1)} %light.1.scale, ...), custom_call_target="tpu_custom_call" | custom-call | flops 3000000 | bytes 12000000 | tf_op jit(solution)/shard_map/finish/pallas_call | solution.py:616
  137.3 1.9 %collective-permute-done.10.other = f32[4,128,256]{2,1,0:T(8,128)S(1)} collective-permute-done((f32[4,128,256]{2,1,0:T(8,128)S(1)}, f32[4,128,256]{2,1,0:T(8,128)S(1)}, u32[]{:S(2)}, u32[]{:S(2)}) %collective-permute-start.10) | collective-permute-done | bytes 524320 | tf_op jit(solution)/shard_map/ppermute | solution.py:644
  139.2 1.0 join.3
  (48 shorter events, 4.3 us)
Async XLA Ops:
  2.8 6.9 %copy-start.7 = (s32[8,2]{0,1:T(2,128)S(1)}, s32[8,2]{0,1:T(2,128)}, u32[]{:S(2)}) copy-start(s32[8,2]{0,1:T(2,128)} %param.12) | copy-start | bytes 196
  2.9 17.8 %collective-permute-start = (f32[2,256,256]{2,1,0:T(8,128)}, f32[2,256,256]{2,1,0:T(8,128)S(1)}, u32[]{:S(2)}, u32[]{:S(2)}) collective-permute-start(f32[2,256,256]{2,1,0:T(8,128)} %get-tuple-element.34), channel_id=1, source_target_pairs={{1,0},{2,1},{3,2},{4,3},{5,4},{6,5},{7,6},{9,8},{10,9},{11,10},{12... | collective-permute-start | bytes 1572872 | tf_op jit(solution)/shard_map/ppermute | solution.py:639
  4.2 26.9 %collective-permute-start.2 = (f32[2,256,256]{2,1,0:T(8,128)}, f32[2,256,256]{2,1,0:T(8,128)S(1)}, u32[]{:S(2)}, u32[]{:S(2)}) collective-permute-start(f32[2,256,256]{2,1,0:T(8,128)} %get-tuple-element.40), channel_id=1, source_target_pairs={{1,0},{2,1},{3,2},{4,3},{5,4},{6,5},{7,6},{9,8},{10,9},{11,10},{12... | collective-permute-start | bytes 1572872 | tf_op jit(solution)/shard_map/ppermute | solution.py:639
  7.7 14.3 %collective-permute-start.1 = (f32[2,256,512]{2,1,0:T(8,128)}, f32[2,256,512]{2,1,0:T(8,128)S(1)}, u32[]{:S(2)}, u32[]{:S(2)}) collective-permute-start(f32[2,256,512]{2,1,0:T(8,128)} %cut_lower.1), channel_id=1, source_target_pairs={{8,0},{16,8},{24,16},{9,1},{17,9},{25,17},{10,2},{18,10},{26,18},{... | collective-permute-start | bytes 3145736 | tf_op jit(solution)/shard_map/ppermute | solution.py:639
  10.0 12.0 %copy-start = (f32[2,2,256,256]{3,2,1,0:T(8,128)S(1)}, f32[2,2,256,256]{3,2,1,0:T(8,128)}, u32[]{:S(2)}) copy-start(f32[2,2,256,256]{3,2,1,0:T(8,128)} %probe.1) | copy-start | bytes 3145732
  13.4 18.5 %copy-start.1 = (f32[2,2,256,256]{3,2,1,0:T(8,128)S(1)}, f32[2,2,256,256]{3,2,1,0:T(8,128)}, u32[]{:S(2)}) copy-start(f32[2,2,256,256]{3,2,1,0:T(8,128)} %probe.1) | copy-start | bytes 3145732
  20.7 9.5 %copy-start.3 = (f32[2,256,256]{2,1,0:T(8,128)}, f32[2,256,256]{2,1,0:T(8,128)S(1)}, u32[]{:S(2)}) copy-start(f32[2,256,256]{2,1,0:T(8,128)S(1)} %collective-permute-done.refs_5_) | copy-start | bytes 1572868
  20.7 11.2 %collective-permute-start.3 = (f32[2,256,256]{2,1,0:T(8,128)S(1)}, f32[2,256,256]{2,1,0:T(8,128)S(1)}, u32[]{:S(2)}, u32[]{:S(2)}) collective-permute-start(f32[2,256,256]{2,1,0:T(8,128)S(1)} %collective-permute-done.refs_5_), channel_id=1, source_target_pairs={{8,0},{16,8},{24,16},{9,1},{17,9},{25,17},{10,2},{18,10},{26,18},{... | collective-permute-start | bytes 1572872 | tf_op jit(solution)/shard_map/ppermute | solution.py:639
  31.1 0.8 copy-start.5
  31.9 1.0 copy-start.4
  32.9 1.0 copy-start.6
  43.7 37.6 %collective-permute-start.7 = (f32[2,264,768]{2,1,0:T(8,128)}, f32[2,264,768]{2,1,0:T(8,128)S(1)}, u32[]{:S(2)}, u32[]{:S(2)}) collective-permute-start(f32[2,264,768]{2,1,0:T(8,128)} %get-tuple-element.52), channel_id=1, source_target_pairs={{0,8},{8,16},{16,24},{1,9},{9,17},{17,25},{2,10},{10,18},{18,26},{... | collective-permute-start | bytes 4866056 | tf_op jit(solution)/shard_map/ppermute | solution.py:639
  49.3 20.8 %collective-permute-start.4 = (f32[5,128,256]{2,1,0:T(8,128)}, f32[5,128,256]{2,1,0:T(8,128)}, u32[]{:S(2)}, u32[]{:S(2)}) collective-permute-start(f32[5,128,256]{2,1,0:T(8,128)} %pick.1), channel_id=1, source_target_pairs={{0,8},{8,0},{16,24},{24,16},{1,9},{9,1},{17,25},{25,17},{2,10},{10... | collective-permute-start | bytes 1966088 | tf_op jit(solution)/shard_map/ppermute | solution.py:644
  68.0 13.3 %collective-permute-start.6 = (f32[2,256,256]{2,1,0:T(8,128)}, f32[2,256,256]{2,1,0:T(8,128)}, u32[]{:S(2)}, u32[]{:S(2)}) collective-permute-start(f32[2,256,256]{2,1,0:T(8,128)} %get-tuple-element.51), channel_id=1, source_target_pairs={{0,1},{1,2},{2,3},{3,4},{4,5},{5,6},{6,7},{8,9},{9,10},{10,11},{11... | collective-permute-start | bytes 1572872 | tf_op jit(solution)/shard_map/ppermute | solution.py:639
  71.3 10.0 %collective-permute-start.5 = (f32[5,64,256]{2,1,0:T(8,128)S(1)}, f32[5,64,256]{2,1,0:T(8,128)S(1)}, u32[]{:S(2)}, u32[]{:S(2)}) collective-permute-start(f32[5,64,256]{2,1,0:T(8,128)S(1)} %get-tuple-element.50), channel_id=1, source_target_pairs={{0,16},{8,24},{16,0},{24,8},{1,17},{9,25},{17,1},{25,9},{2,18},{10... | collective-permute-start | bytes 983048 | tf_op jit(solution)/shard_map/ppermute | solution.py:644
  82.1 12.3 %all-to-all-start = ((f32[8,5,8,256]{3,2,1,0:T(8,128)}), f32[8,5,8,256]{3,2,1,0:T(8,128)S(1)}, u32[]{:S(2)}, u32[]{:S(2)}) async-start(f32[8,5,8,256]{3,2,1,0:T(8,128)} %copy_bitcast_fusion), calls=%async_computation | async-start | bytes 655360 | tf_op jit(solution)/shard_map/all_to_all | solution.py:829
  85.9 11.1 %collective-permute-start.8 = (f32[2,264,256]{2,1,0:T(8,128)S(1)}, f32[2,264,256]{2,1,0:T(8,128)S(1)}, u32[]{:S(2)}, u32[]{:S(2)}) collective-permute-start(f32[2,264,256]{2,1,0:T(8,128)S(1)} %merge.1), channel_id=1, source_target_pairs={{0,1},{1,2},{2,3},{3,4},{4,5},{5,6},{6,7},{8,9},{9,10},{10,11},{11... | collective-permute-start | bytes 1622024 | tf_op jit(solution)/shard_map/ppermute | solution.py:639
  97.8 14.5 %all-to-all-start.1 = ((f32[8,4,8,256]{3,2,1,0:T(8,128)}), f32[8,4,8,256]{3,2,1,0:T(8,128)S(1)}, u32[]{:S(2)}, u32[]{:S(2)}) async-start(f32[8,4,8,256]{3,2,1,0:T(8,128)} %broadcast_in_dim.2), calls=%async_computation.1 | async-start | bytes 524288 | tf_op jit(solution)/shard_map/all_to_all | solution.py:836
  112.3 24.8 %collective-permute-start.9 = (f32[4,64,256]{2,1,0:T(8,128)S(1)}, f32[4,64,256]{2,1,0:T(8,128)S(1)}, u32[]{:S(2)}, u32[]{:S(2)}) collective-permute-start(f32[4,64,256]{2,1,0:T(8,128)S(1)} %copy_bitcast_fusion.1.mine), channel_id=1, source_target_pairs={{0,16},{8,24},{16,0},{24,8},{1,17},{9,25},{17,1},{25,9},{2,18},{10... | collective-permute-start | bytes 786440 | tf_op jit(solution)/shard_map/ppermute | solution.py:644
  130.8 1.2 copy-start.2
  137.2 2.0 %collective-permute-start.10 = (f32[4,128,256]{2,1,0:T(8,128)S(1)}, f32[4,128,256]{2,1,0:T(8,128)S(1)}, u32[]{:S(2)}, u32[]{:S(2)}) collective-permute-start(f32[4,128,256]{2,1,0:T(8,128)S(1)} %join.2.mine), channel_id=1, source_target_pairs={{0,8},{8,0},{16,24},{24,16},{1,9},{9,1},{17,25},{25,17},{2,10},{10... | collective-permute-start | bytes 1572872 | tf_op jit(solution)/shard_map/ppermute | solution.py:644
